TPU v7x, 32 devices: a whole 2x2x4 slice. The times are simulated.
32 devices in a mesh: dp: 4 (over z), expert: 8 (over y, x, core).
Axes of the slice: x: 2, y: 2, z: 4, core: 2. Of those that a mesh axis runs over, the one named last changes fastest.
Arguments:
- tokens: bfloat16 [16384, 1024], P(('dp', 'expert')), may hold values from -12 to 12
- lengths: int32 [32, 2], P(('dp', 'expert')), may hold values from 1 to 448, 512 in all within a row
- routes: int32 [16384, 2], P(('dp', 'expert')), may hold values from 0 to 7, all different within a row; in each aligned block of 512 rows (0 to 511, 512 to 1023, ...) at most 256 rows name the same one
- cotangent: bfloat16 [16384, 1024], P(('dp', 'expert')), may hold values from -6 to 6
- gain_attn: bfloat16 [1024], P('dp'), may hold values from 0.5 to 1.5
- w_query: bfloat16 [1024, 1024], P('dp'), may hold values from -0.1875 to 0.1875
- key_projection_weight: bfloat16 [1024, 512], P('dp'), may hold values from -0.1875 to 0.1875
- value_projection_weight: bfloat16 [1024, 512], P('dp'), may hold values from -0.1875 to 0.1875
- w_out: bfloat16 [1024, 1024], P('dp'), may hold values from -1 to 1
- gain_moe: bfloat16 [1024], P('dp'), may hold values from 0.5 to 1.5
- w_router: bfloat16 [1024, 8], P('dp'), may hold values from -0.09375 to 0.09375
- w_gate: bfloat16 [8, 1024, 512], P('expert'), may hold values from -0.1875 to 0.1875
- w_up: bfloat16 [8, 1024, 512], P('expert'), may hold values from -0.1875 to 0.1875
- w_down: bfloat16 [8, 512, 1024], P('expert'), may hold values from -0.75 to 0.75
Outputs:
- mixed: bfloat16 [16384, 1024], P(('dp', 'expert'))
- grad_tokens: bfloat16 [16384, 1024], P(('dp', 'expert'))
- grad_gain_attn: float32 [1024], P('dp')
- grad_query: float32 [1024, 1024], P('dp')
- key_matrix_gradient: float32 [1024, 512], P('dp')
- value_matrix_gradient: float32 [1024, 512], P('dp')
- grad_out: float32 [1024, 1024], P('dp')
- grad_gain_moe: float32 [1024], P('dp')
- grad_router: float32 [1024, 8], P('dp')
- grad_gate: float32 [8, 1024, 512], P('expert', 'dp')
- grad_up: float32 [8, 1024, 512], P('expert', 'dp')
- grad_down: float32 [8, 512, 1024], P('expert', 'dp')
Inputs may be any that keep to these rules, and one draw needn't show every extreme that they name: In the 512 rows of one device no expert is named by more than 256 routes, a bound that some block reaches; a token's 2 experts differ. Each device's 2 lengths sum to 512; its longest is at most 448.
All inputs are finite; a program needn't handle non-finite values.
Results may differ from a plain program's by a relative error of at most 0.023.
Values may be sent and summed in bfloat16 or wider, within the bound.
No kernel may reach another device: no remote copies, remote signals or barrier semaphores. Data moves between devices by JAX's collectives and lax.ppermute only.
A program may use at most 256 MiB of HBM per device.

v0:
```python
import math

import jax
import jax.numpy as jnp
from jax import lax
from jax.sharding import PartitionSpec as P

QUERY_HEADS = 16
KEY_VALUE_HEADS = 8
HEAD_DIMENSION = 64


eps_norm = 1e-06


def as_sent(shard):
    return jax.tree.map(lambda a: a.astype(jnp.bfloat16) if a.dtype == jnp.float32 else a, shard)


def positions_of(lengths_row, count_of_rows):
    index_rows = jnp.arange(count_of_rows, dtype=jnp.int32)
    ends = jnp.cumsum(lengths_row)
    member = jnp.sum((index_rows[:, None] >= ends[None, :]).astype(jnp.int32), axis=1)
    starts = ends - lengths_row
    onehot = member[:, None] == jnp.arange(lengths_row.shape[0], dtype=jnp.int32)[None, :]
    begin = jnp.sum(jnp.where(onehot, starts[None, :], 0), axis=1)
    return (member, index_rows - begin)


def rope_tables(positions, head_size):
    half_size = head_size // 2
    freq = jnp.exp(
        jnp.arange(half_size, dtype=jnp.float32) * (-2.0 * math.log(10000.0) / head_size)
    )
    angle = positions.astype(jnp.float32)[:, None] * freq[None, :]
    return (jnp.cos(angle), jnp.sin(angle))


def apply_rotary(values, cosine_table, sine_table):
    half_size = values.shape[-1] // 2
    first = values[..., :half_size]
    second = values[..., half_size:]
    cos_b = cosine_table[:, None, :]
    sin_b = sine_table[:, None, :]
    return jnp.concatenate(
        [first * cos_b - second * sin_b, second * cos_b + first * sin_b], axis=-1
    )


def reverse_rotary(grads, cosine_table, sine_table):
    half_size = grads.shape[-1] // 2
    first = grads[..., :half_size]
    second = grads[..., half_size:]
    cos_b = cosine_table[:, None, :]
    sin_b = sine_table[:, None, :]
    return jnp.concatenate(
        [first * cos_b + second * sin_b, second * cos_b - first * sin_b], axis=-1
    )


def local(
    tokens,
    lengths,
    routes,
    cotangent,
    gain_attn,
    w_query,
    key_projection_weight,
    value_projection_weight,
    w_out,
    gain_moe,
    w_router,
    w_gate,
    w_up,
    w_down,
):
    single_float = jnp.float32
    brain_float_half = jnp.bfloat16
    count_of_rows, model_width = tokens.shape
    expert_count = lax.axis_size("expert")
    top_count = routes.shape[1]
    capacity = 2 * count_of_rows * top_count // expert_count
    group_factor = QUERY_HEADS // KEY_VALUE_HEADS
    scale = HEAD_DIMENSION ** (-0.5)
    gain_one, query_w, key_weight_local, value_weight_local, out_w, gain_two, router_w = (
        lax.all_gather(gain_attn, "dp", axis=0, tiled=True),
        lax.all_gather(w_query, "dp", axis=0, tiled=True),
        lax.all_gather(key_projection_weight, "dp", axis=0, tiled=True),
        lax.all_gather(value_projection_weight, "dp", axis=0, tiled=True),
        lax.all_gather(w_out, "dp", axis=0, tiled=True),
        lax.all_gather(gain_moe, "dp", axis=0, tiled=True),
        lax.all_gather(w_router, "dp", axis=0, tiled=True),
    )
    gain_first = gain_one.astype(single_float)
    gain_second = gain_two.astype(single_float)
    resid_in = tokens.astype(single_float)
    inverse_one = lax.rsqrt(jnp.mean(resid_in * resid_in, axis=-1, keepdims=True) + eps_norm)
    first_normalized = (resid_in * inverse_one * gain_first).astype(brain_float_half)
    query_before_rotation = jnp.dot(
        first_normalized, query_w, preferred_element_type=single_float
    ).reshape(count_of_rows, QUERY_HEADS, HEAD_DIMENSION)
    key_before_rotation = jnp.dot(
        first_normalized, key_weight_local, preferred_element_type=single_float
    ).reshape(count_of_rows, KEY_VALUE_HEADS, HEAD_DIMENSION)
    value_before_mixing = jnp.dot(
        first_normalized, value_weight_local, preferred_element_type=single_float
    )
    member, position = positions_of(lengths[0], count_of_rows)
    cosine_table, sine_table = rope_tables(position, HEAD_DIMENSION)
    query_vectors = (
        apply_rotary(query_before_rotation, cosine_table, sine_table)
        .astype(brain_float_half)
        .reshape(count_of_rows, KEY_VALUE_HEADS, group_factor, HEAD_DIMENSION)
    )
    key_row_block = apply_rotary(key_before_rotation, cosine_table, sine_table).astype(
        brain_float_half
    )
    value_row_block = value_before_mixing.astype(brain_float_half).reshape(
        count_of_rows, KEY_VALUE_HEADS, HEAD_DIMENSION
    )
    index_rows = jnp.arange(count_of_rows, dtype=jnp.int32)
    allowed = (member[:, None] == member[None, :]) & (index_rows[:, None] >= index_rows[None, :])

    def masked_scores():
        raw_scores = (
            jnp.einsum(
                "qcgd,kcd->cgqk", query_vectors, key_row_block, preferred_element_type=single_float
            )
            * scale
        )
        return jnp.where(allowed, raw_scores, -1e30)

    scores = masked_scores()
    row_peak = jnp.max(scores, axis=-1, keepdims=True)
    shifted_exp = jnp.exp(scores - row_peak)
    row_total = jnp.sum(shifted_exp, axis=-1, keepdims=True)
    probs = (shifted_exp / row_total).astype(brain_float_half)
    log_total = row_peak + jnp.log(row_total)
    mixed_heads = jnp.einsum(
        "cgqk,kcd->qcgd", probs, value_row_block, preferred_element_type=single_float
    )
    attn_rows = mixed_heads.reshape(count_of_rows, QUERY_HEADS * HEAD_DIMENSION).astype(
        brain_float_half
    )
    resid_mid = resid_in + jnp.dot(attn_rows, out_w, preferred_element_type=single_float)
    inverse_two = lax.rsqrt(jnp.mean(resid_mid * resid_mid, axis=-1, keepdims=True) + eps_norm)
    normed_two = (resid_mid * inverse_two * gain_second).astype(brain_float_half)
    logits = jnp.dot(normed_two, router_w, preferred_element_type=single_float)
    expert_ids = jnp.arange(expert_count, dtype=jnp.int32)
    chosen = (routes[:, :, None] == expert_ids[None, None, :]).astype(single_float)
    picked = jnp.einsum("te,tke->tk", logits, chosen)
    gates = jax.nn.softmax(picked, axis=-1)
    flat_routes = routes.reshape(-1)
    route_count = flat_routes.shape[0]
    hits = (flat_routes[:, None] == expert_ids[None, :]).astype(jnp.int32)
    earlier = jnp.cumsum(hits, axis=0) - hits
    target = flat_routes * capacity + jnp.sum(earlier * hits, axis=1)
    slot_route = (
        jnp.full((expert_count * capacity,), route_count, jnp.int32)
        .at[target]
        .set(jnp.arange(route_count, dtype=jnp.int32))
    )
    padded_two = jnp.concatenate(
        [normed_two, jnp.zeros((1, model_width), brain_float_half)], axis=0
    )
    outgoing = jnp.take(padded_two, slot_route // top_count, axis=0).reshape(
        expert_count, capacity, model_width
    )
    gate_mat = w_gate[0]
    up_mat = w_up[0]
    down_mat = w_down[0]
    received = lax.all_to_all(outgoing, "expert", split_axis=0, concat_axis=0, tiled=True)
    flat_in = received.reshape(-1, model_width)
    gate_pre = jnp.dot(flat_in, gate_mat, preferred_element_type=single_float)
    up_pre = jnp.dot(flat_in, up_mat, preferred_element_type=single_float)
    hidden = (jax.nn.silu(gate_pre) * up_pre).astype(brain_float_half)
    result = (
        jnp.dot(hidden, down_mat, preferred_element_type=single_float)
        .astype(brain_float_half)
        .reshape(received.shape)
    )
    returned = lax.all_to_all(result, "expert", split_axis=0, concat_axis=0, tiled=True)
    expert_out = jnp.take(returned.reshape(-1, model_width), target, axis=0).reshape(
        count_of_rows, top_count, model_width
    )
    moe = jnp.einsum("tk,tkd->td", gates, expert_out, preferred_element_type=single_float)
    mixed_out = (resid_mid + moe).astype(brain_float_half)
    grad_final = cotangent.astype(single_float)
    grad_gates = jnp.einsum(
        "tkd,td->tk", expert_out, cotangent, preferred_element_type=single_float
    )
    grad_picked = gates * (grad_gates - jnp.sum(gates * grad_gates, axis=-1, keepdims=True))
    grad_logits = jnp.einsum("tk,tke->te", grad_picked, chosen).astype(brain_float_half)
    grad_router_w = jnp.dot(normed_two.T, grad_logits, preferred_element_type=single_float)
    grad_normed_two = jnp.dot(grad_logits, router_w.T, preferred_element_type=single_float)
    grad_expert_out = (
        (gates[:, :, None] * grad_final[:, None, :])
        .astype(brain_float_half)
        .reshape(route_count, model_width)
    )
    padded_grad = jnp.concatenate(
        [grad_expert_out, jnp.zeros((1, model_width), brain_float_half)], axis=0
    )
    outgoing_grad = jnp.take(padded_grad, slot_route, axis=0).reshape(
        expert_count, capacity, model_width
    )
    arrived_grad = lax.all_to_all(outgoing_grad, "expert", split_axis=0, concat_axis=0, tiled=True)
    flat_in = received.reshape(-1, model_width)
    flat_grad = arrived_grad.reshape(-1, model_width)
    gate_pre = jnp.dot(flat_in, gate_mat, preferred_element_type=single_float)
    up_pre = jnp.dot(flat_in, up_mat, preferred_element_type=single_float)
    sigm_gate = jax.nn.sigmoid(gate_pre)
    activated = jax.nn.silu(gate_pre)
    hidden = (activated * up_pre).astype(brain_float_half)
    grad_down_w = jnp.dot(hidden.T, flat_grad, preferred_element_type=single_float)
    grad_hidden = jnp.dot(flat_grad, down_mat.T, preferred_element_type=single_float)
    grad_gate_pre = (
        grad_hidden * up_pre * sigm_gate * (1.0 + gate_pre * (1.0 - sigm_gate))
    ).astype(brain_float_half)
    grad_up_pre = (grad_hidden * activated).astype(brain_float_half)
    grad_gate_w = jnp.dot(flat_in.T, grad_gate_pre, preferred_element_type=single_float)
    grad_up_w = jnp.dot(flat_in.T, grad_up_pre, preferred_element_type=single_float)
    grad_flat_in = jnp.dot(
        grad_gate_pre, gate_mat.T, preferred_element_type=single_float
    ) + jnp.dot(grad_up_pre, up_mat.T, preferred_element_type=single_float)
    grad_send = grad_flat_in.astype(brain_float_half).reshape(expert_count, capacity, model_width)
    grad_back = lax.all_to_all(grad_send, "expert", split_axis=0, concat_axis=0, tiled=True)
    grad_routes = jnp.take(grad_back.reshape(-1, model_width), target, axis=0).reshape(
        count_of_rows, top_count, model_width
    )
    grad_normed_two = grad_normed_two + jnp.sum(grad_routes, axis=1, dtype=single_float)
    scaled_two = grad_normed_two * gain_second
    grad_gain_two = jnp.sum(grad_normed_two * resid_mid * inverse_two, axis=0)
    grad_mid = (
        grad_final
        + inverse_two * scaled_two
        - resid_mid
        * inverse_two
        * inverse_two
        * inverse_two
        * jnp.mean(resid_mid * scaled_two, axis=-1, keepdims=True)
    )
    grad_mid_low = grad_mid.astype(brain_float_half)
    grad_out_w = jnp.dot(attn_rows.T, grad_mid_low, preferred_element_type=single_float)
    grad_attn = (
        jnp.dot(grad_mid_low, out_w.T, preferred_element_type=single_float)
        .astype(brain_float_half)
        .reshape(count_of_rows, KEY_VALUE_HEADS, group_factor, HEAD_DIMENSION)
    )
    scores_again = masked_scores()
    probs_again = jnp.exp(scores_again - log_total)
    grad_probs = jnp.einsum(
        "qcgd,kcd->cgqk", grad_attn, value_row_block, preferred_element_type=single_float
    )
    delta_rows = jnp.sum(probs_again * grad_probs, axis=-1, keepdims=True)
    grad_scores = (probs_again * (grad_probs - delta_rows)).astype(brain_float_half)
    grad_query = (
        jnp.einsum(
            "cgqk,kcd->qcgd", grad_scores, key_row_block, preferred_element_type=single_float
        )
        * scale
    ).reshape(count_of_rows, QUERY_HEADS, HEAD_DIMENSION)
    key_matrix_gradient = (
        jnp.einsum(
            "cgqk,qcgd->kcd", grad_scores, query_vectors, preferred_element_type=single_float
        )
        * scale
    )
    value_matrix_gradient = jnp.einsum(
        "cgqk,qcgd->kcd",
        probs_again.astype(brain_float_half),
        grad_attn,
        preferred_element_type=single_float,
    )
    grad_query_pre = (
        reverse_rotary(grad_query, cosine_table, sine_table)
        .reshape(count_of_rows, QUERY_HEADS * HEAD_DIMENSION)
        .astype(brain_float_half)
    )
    key_before_gradient = (
        reverse_rotary(key_matrix_gradient, cosine_table, sine_table)
        .reshape(count_of_rows, KEY_VALUE_HEADS * HEAD_DIMENSION)
        .astype(brain_float_half)
    )
    value_before_gradient = value_matrix_gradient.reshape(
        count_of_rows, KEY_VALUE_HEADS * HEAD_DIMENSION
    ).astype(brain_float_half)
    grad_query_w = jnp.dot(first_normalized.T, grad_query_pre, preferred_element_type=single_float)
    grad_key_w = jnp.dot(
        first_normalized.T, key_before_gradient, preferred_element_type=single_float
    )
    grad_value_w = jnp.dot(
        first_normalized.T, value_before_gradient, preferred_element_type=single_float
    )
    grad_normed_one = jnp.dot(grad_query_pre, query_w.T, preferred_element_type=single_float)
    grad_normed_one = grad_normed_one + jnp.dot(
        key_before_gradient, key_weight_local.T, preferred_element_type=single_float
    )
    grad_normed_one = grad_normed_one + jnp.dot(
        value_before_gradient, value_weight_local.T, preferred_element_type=single_float
    )
    scaled_one = grad_normed_one * gain_first
    grad_gain_one = jnp.sum(grad_normed_one * resid_in * inverse_one, axis=0)
    grad_input = (
        grad_mid
        + inverse_one * scaled_one
        - resid_in
        * inverse_one
        * inverse_one
        * inverse_one
        * jnp.mean(resid_in * scaled_one, axis=-1, keepdims=True)
    )
    gate_three = grad_gate_w[None]
    up_three = grad_up_w[None]
    down_three = grad_down_w[None]
    local_parts = (
        lax.psum_scatter(
            grad_gain_one.astype(jnp.bfloat16), "dp", scatter_dimension=0, tiled=True
        ).astype(jnp.float32),
        lax.psum_scatter(
            grad_query_w.astype(jnp.bfloat16), "dp", scatter_dimension=0, tiled=True
        ).astype(jnp.float32),
        lax.psum_scatter(
            grad_key_w.astype(jnp.bfloat16), "dp", scatter_dimension=0, tiled=True
        ).astype(jnp.float32),
        lax.psum_scatter(
            grad_value_w.astype(jnp.bfloat16), "dp", scatter_dimension=0, tiled=True
        ).astype(jnp.float32),
        lax.psum_scatter(
            grad_out_w.astype(jnp.bfloat16), "dp", scatter_dimension=0, tiled=True
        ).astype(jnp.float32),
        lax.psum_scatter(
            grad_gain_two.astype(jnp.bfloat16), "dp", scatter_dimension=0, tiled=True
        ).astype(jnp.float32),
        lax.psum_scatter(
            grad_router_w.astype(jnp.bfloat16), "dp", scatter_dimension=0, tiled=True
        ).astype(jnp.float32),
        lax.psum_scatter(
            gate_three.astype(jnp.bfloat16), "dp", scatter_dimension=1, tiled=True
        ).astype(jnp.float32),
        lax.psum_scatter(
            up_three.astype(jnp.bfloat16), "dp", scatter_dimension=1, tiled=True
        ).astype(jnp.float32),
        lax.psum_scatter(
            down_three.astype(jnp.bfloat16), "dp", scatter_dimension=1, tiled=True
        ).astype(jnp.float32),
    )
    shared_parts = jax.tree.map(
        lambda part: part.astype(jnp.float32), lax.psum(as_sent(tuple(local_parts[:7])), "expert")
    )
    expert_parts = tuple(local_parts[7:])
    return (
        mixed_out,
        grad_input.astype(brain_float_half),
        shared_parts[0],
        shared_parts[1],
        shared_parts[2],
        shared_parts[3],
        shared_parts[4],
        shared_parts[5],
        shared_parts[6],
        expert_parts[0],
        expert_parts[1],
        expert_parts[2],
    )


def solution(mesh):
    placed = (
        P(("dp", "expert"), None),
        P(("dp", "expert"), None),
        P(("dp", "expert"), None),
        P(("dp", "expert"), None),
        P("dp"),
        P("dp", None),
        P("dp", None),
        P("dp", None),
        P("dp", None),
        P("dp"),
        P("dp", None),
        P("expert", None, None),
        P("expert", None, None),
        P("expert", None, None),
    )
    return jax.shard_map(
        local,
        mesh=mesh,
        in_specs=placed,
        out_specs=(
            P(("dp", "expert"), None),
            P(("dp", "expert"), None),
            P("dp"),
            P("dp", None),
            P("dp", None),
            P("dp", None),
            P("dp", None),
            P("dp"),
            P("dp", None),
            P("expert", "dp", None),
            P("expert", "dp", None),
            P("expert", "dp", None),
        ),
        check_vma=False,
    )
```

profile of v0, /device:TPU:0, one launch (start us, length us, event | category | flops | bytes accessed | tf_op | source)
XLA Modules:
  0.0 754.8 jit_solution(547172114617059136)
XLA Ops:
  15.7 4.3 scatter_custom_fusion
  22.8 12.7 %all-gather.1 = bf16[4,1,256]{2,1,0:T(2,128)(2,1)S(1)} all-gather(bf16[1,1,256]{2,1,0:T(2,128)(2,1)S(1)} %reshape.335), channel_id=1, replica_groups=mesh['dp'=4,'expert'=8] {'dp'}, dimensions={0}, use_global_device_ids=true | all-gather | bytes 2560 | tf_op jit(solution)/shard_map/all_gather | solution.py:91
  36.1 8.1 %all-gather = bf16[4,1,256]{2,1,0:T(2,128)(2,1)S(1)} all-gather(bf16[1,1,256]{2,1,0:T(2,128)(2,1)S(1)} %reshape.333), channel_id=1, replica_groups=mesh['dp'=4,'expert'=8] {'dp'}, dimensions={0}, use_global_device_ids=true | all-gather | bytes 2560 | tf_op jit(solution)/shard_map/all_gather | solution.py:86
  48.2 21.2 %all-gather.7.cloned.1.call-done = bf16[1024,512]{1,0:T(8,128)(2,1)} async-done(((bf16[256,512]{1,0:T(8,128)(2,1)}), bf16[1024,512]{1,0:T(8,128)(2,1)}) %all-gather.7.cloned.1.call-update) | async-done | bytes 1048592 | tf_op jit(solution)/shard_map/all_gather | solution.py:89
  72.3 44.2 %all-gather.11.cloned.1.call-done = bf16[1024,1024]{1,0:T(8,128)(2,1)} async-done(((bf16[256,1024]{1,0:T(8,128)(2,1)}), bf16[1024,1024]{1,0:T(8,128)(2,1)}) %all-gather.11.cloned.1.call-update) | async-done | bytes 2097168 | tf_op jit(solution)/shard_map/all_gather | solution.py:87
  120.6 7.5 fusion.81
  128.2 8.3 %fusion.3 = f32[8,2,512]{2,1,0:T(2,128)S(1)} fusion(f32[8,2,512,512]{2,3,1,0:T(8,128)} %get-tuple-element.47, f32[8,2,512]{2,1,0:T(2,128)S(1)} %get-tuple-element.46), kind=kLoop, calls=%fused_computation.14 | loop fusion | flops 8380416 | bytes 16842752 | tf_op jit(solution)/shard_map/reduce_sum | solution.py:136
  136.5 7.6 %fusion.24 = bf16[8,64,2,512]{3,1,2,0:T(8,128)(2,1)S(1)} fusion(bf16[512,8,64,1]{0,2,3,1:T(8,128)(2,1)S(1)} %bitcast.221, f32[8,2,512,512]{2,3,1,0:T(8,128)} %get-tuple-element.47, f32[8,2,512]{2,1,0:T(2,128)S(1)} %fusion.3, f32[8,2,512]{2,1,0:T(2,128)S(1)} %get-tuple-element.46), kind=kOutput, calls=%fused_computation.61 | convolution fusion | flops 549978112 | bytes 18415616 | tf_op jit(solution)/shard_map/cgqk,kcd->qcgd/dot_general | solution.py:139
  144.1 18.5 %all-gather.13.cloned.1.call-done = bf16[1024,1024]{1,0:T(8,128)(2,1)} async-done(((bf16[256,1024]{1,0:T(8,128)(2,1)}), bf16[1024,1024]{1,0:T(8,128)(2,1)}) %all-gather.13.cloned.1.call-update) | async-done | bytes 2097168 | tf_op jit(solution)/shard_map/all_gather | solution.py:90
  166.9 9.6 %gather_fusion = bf16[2048,1024]{1,0:T(8,128)(2,1)} fusion(bf16[513,1024]{1,0:T(8,128)(2,1)S(1)} %concatenate.31, s32[2048]{0:T(1024)S(1)} %copy-done.58), kind=kCustom, calls=%fused_computation.2 | custom fusion | bytes 8396800 | tf_op jit(solution)/shard_map/jit(_take)/gather | solution.py:166
  179.1 52.8 %all_to_all.20 = bf16[8,256,1024]{2,1,0:T(8,128)(2,1)S(1)} all-to-all(bf16[8,256,1024]{2,1,0:T(8,128)(2,1)S(1)} %broadcast_select_fusion.1), channel_id=1, replica_groups=mesh['dp'=4,'expert'=8] {'expert'}, dimensions={0} | all-to-all | bytes 8388608 | tf_op jit(solution)/shard_map/all_to_all | solution.py:172
  234.3 5.1 multiply_convert_fusion.3
  239.4 4.4 convolution_convert_fusion
  243.8 4.7 all-to-all-start.1
  251.7 6.1 mul.412
  257.8 13.3 %all_gather.27 = bf16[1024,8]{0,1:T(8,128)(2,1)S(1)} all-gather(bf16[256,8]{0,1:T(8,128)(2,1)S(1)} %copy-done.66), channel_id=1, replica_groups=mesh['dp'=4,'expert'=8] {'dp'}, dimensions={0}, use_global_device_ids=true | all-gather | bytes 20480 | tf_op jit(solution)/shard_map/all_gather | solution.py:92
  273.7 23.9 %all-to-all-done.1 = bf16[8,256,1024]{2,1,0:T(8,128)(2,1)} async-done(((bf16[8,256,1024]{2,1,0:T(8,128)(2,1)}), bf16[8,256,1024]{2,1,0:T(8,128)(2,1)}, u32[]{:S(2)}, u32[]{:S(2)}) %all-to-all-start.1) | async-done | bytes 4194336 | tf_op jit(solution)/shard_map/all_to_all | solution.py:182
  297.6 7.7 %gather_fusion.2 = bf16[1024,1024]{1,0:T(8,128)(2,1)S(1)} fusion(bf16[2048,1024]{1,0:T(8,128)(2,1)} %bitcast.32, s32[1024]{0:T(1024)S(1)} %broadcast_clamp_fusion.1), kind=kCustom, calls=%fused_computation.clone | custom fusion | bytes 4198400 | tf_op jit(solution)/shard_map/jit(_take)/gather | solution.py:183
  307.0 4.2 reshape.282
  311.2 5.9 fusion.22
  321.0 9.6 %gather_fusion.1 = bf16[2048,1024]{1,0:T(8,128)(2,1)} fusion(bf16[1025,1024]{1,0:T(8,128)(2,1)S(1)} %concatenate.32, s32[2048]{0:T(1024)S(1)} %copy-done.57), kind=kCustom, calls=%fused_computation.3 | custom fusion | bytes 8396800 | tf_op jit(solution)/shard_map/jit(_take)/gather | solution.py:204
  333.1 52.1 %all_to_all.21 = bf16[8,256,1024]{2,1,0:T(8,128)(2,1)S(1)} all-to-all(bf16[8,256,1024]{2,1,0:T(8,128)(2,1)S(1)} %broadcast_select_fusion), channel_id=1, replica_groups=mesh['dp'=4,'expert'=8] {'expert'}, dimensions={0} | all-to-all | bytes 8388608 | tf_op jit(solution)/shard_map/all_to_all | solution.py:207
  387.2 3.4 fusion.27
  390.6 8.6 %multiply_convert_fusion = (bf16[2048,512]{1,0:T(8,128)(2,1)}, bf16[2048,512]{1,0:T(8,128)(2,1)}) fusion(f32[2048,512]{1,0:T(8,128)} %copy-done.80, f32[2048,512]{1,0:T(8,128)} %get-tuple-element.51, bf16[2048,1024]{1,0:T(8,128)(2,1)} %bitcast.198, bf16[1,512,1024]{2,1,0:T(8,128)(2,1)S(1)} %copy-done), kind=kOutput, calls=%fused_computation.20 | convolution fusion | flops 2161115136 | bytes 17825792 | tf_op jit(solution)/shard_map/dot_general | solution.py:216
  399.3 4.2 fusion.42
  403.5 4.6 add_convert_fusion
  408.1 4.7 all-to-all-start.3
  412.9 5.6 fusion.26
  422.0 3.6 fusion.83
  429.0 32.9 %all-to-all-done.3 = bf16[8,256,1024]{2,1,0:T(8,128)(2,1)} async-done(((bf16[8,256,1024]{2,1,0:T(8,128)(2,1)}), bf16[8,256,1024]{2,1,0:T(8,128)(2,1)}, u32[]{:S(2)}, u32[]{:S(2)}) %all-to-all-start.3) | async-done | bytes 4194336 | tf_op jit(solution)/shard_map/all_to_all | solution.py:227
  461.9 7.7 %gather_fusion.3 = bf16[1024,1024]{1,0:T(8,128)(2,1)S(1)} fusion(bf16[2048,1024]{1,0:T(8,128)(2,1)} %bitcast.44, s32[1024]{0:T(1024)S(1)} %broadcast_clamp_fusion.1), kind=kCustom, calls=%fused_computation.1.clone | custom fusion | bytes 4198400 | tf_op jit(solution)/shard_map/jit(_take)/gather | solution.py:228
  472.0 5.8 reshape.288
  477.9 8.7 %reduce_sum.137 = f32[512,1024]{1,0:T(8,128)} reduce(f32[512,2,1024]{2,1,0:T(2,128)} %reshape.288, f32[]{:T(128)} %constant.52.clone.1), dimensions={1}, to_apply=%region_14.16 | reduce | flops 524288 | bytes 6291460 | tf_op jit(solution)/shard_map/reduce_sum | solution.py:231
  495.0 8.5 %fusion.33 = bf16[8,64,512]{2,1,0:T(8,128)(2,1)S(1)} fusion(bf16[512,8,2,64]{0,3,2,1:T(8,128)(2,1)S(1)} %bitcast.187, f32[8,2,512,512]{2,3,1,0:T(8,128)} %get-tuple-element.47, f32[8,2,512]{2,1,0:T(2,128)S(1)} %bitcast.223), kind=kOutput, calls=%fused_computation.75 | convolution fusion | flops 545521664 | bytes 18382848 | tf_op jit(solution)/shard_map/cgqk,qcgd->kcd/dot_general | solution.py:269
  505.5 10.8 %fusion = (f32[8,2,512]{2,1,0:T(2,128)S(1)}, f32[8,512,512,2]{2,1,3,0:T(8,128)}) fusion(f32[8,2,512,512]{2,3,1,0:T(8,128)} %get-tuple-element.47, f32[8,2,512]{2,1,0:T(2,128)S(1)} %bitcast.224, bf16[512,8,64,1]{0,2,3,1:T(8,128)(2,1)S(1)} %bitcast.222, bf16[512,8,2,64]{0,3,2,1:T(8,128)(2,1)S(1)} %bitcast.188), kind=kOutput, calls=%fused_computation.7 | convolution fusion | flops 549445632 | bytes 35192832 | tf_op jit(solution)/shard_map/qcgd,kcd->cgqk/dot_general | solution.py:252
  516.4 12.6 %fusion.2 = bf16[8,2,512,512]{2,3,1,0:T(8,128)(2,1)S(1)} fusion(f32[8,512,512,2]{2,1,3,0:T(8,128)} %get-tuple-element.54, f32[8,2,512,512]{2,3,1,0:T(8,128)} %get-tuple-element.47, f32[8,2,512]{2,1,0:T(2,128)S(1)} %get-tuple-element.53, f32[8,2,512]{2,1,0:T(2,128)S(1)} %bitcast.225), kind=kLoop, calls=%fused_computation.9 | loop fusion | flops 16777216 | bytes 42008576 | tf_op jit(solution)/shard_map/convert_element_type | solution.py:256
  534.5 4.2 convolution_convert_fusion.1
  539.7 4.9 convolution_multiply_fusion
  557.2 4.7 fusion.84
  564.0 5.5 reduce-scatter.11.cloned.1.call-done
  569.4 44.8 %reduce-scatter.15.cloned.1.call-done = bf16[256,1024]{1,0:T(8,128)(2,1)} async-done(((bf16[1024,1024]{1,0:T(8,128)(2,1)}), bf16[256,1024]{1,0:T(8,128)(2,1)}) %reduce-scatter.15.cloned.1.call-update) | async-done | bytes 524304 | tf_op jit(solution)/shard_map/reduce_scatter | solution.py:329
  614.2 45.5 %reduce-scatter.9.cloned.1.call-done = bf16[256,1024]{1,0:T(8,128)(2,1)} async-done(((bf16[1024,1024]{1,0:T(8,128)(2,1)}), bf16[256,1024]{1,0:T(8,128)(2,1)}) %reduce-scatter.9.cloned.1.call-update) | async-done | bytes 524304 | tf_op jit(solution)/shard_map/reduce_scatter | solution.py:320
  659.8 4.7 fusion.20
  664.5 9.8 %all-reduce.6 = (bf16[1024]{0:T(1024)(128)(2,1)S(1)}, bf16[1024]{0:T(1024)(128)(2,1)S(1)}) all-reduce(bf16[1024]{0:T(1024)(128)(2,1)S(1)} %get-tuple-element.15, bf16[1024]{0:T(1024)(128)(2,1)S(1)} %copy-done.63), channel_id=2, replica_groups=mesh['dp'=4,'expert'=8] {'dp'}, use_global_device_ids=true, to_apply=%region_19.21.clone | all-reduce | flops 2048 | bytes 8192
  674.5 6.2 reduce-scatter.17.cloned.1.call-done
  680.8 12.4 %all-reduce.4 = (bf16[256]{0:T(256)(128)(2,1)S(1)}, bf16[256]{0:T(256)(128)(2,1)S(1)}, bf16[256,8]{0,1:T(8,128)(2,1)S(1)}) all-reduce(bf16[256]{0:T(256)(128)(2,1)S(1)} %dynamic-slice.1, bf16[256]{0:T(256)(128)(2,1)S(1)} %dynamic-slice.3, ...), channel_id=1, replica_groups=mesh['dp'=4,'expert'=8] {'expert'}, use_global_device_ids=true, to_apply=%region_20.22 | all-reduce | flops 2560 | bytes 10240 | tf_op jit(solution)/shard_map/psum | solution.py:349
  694.9 4.0 fusion.16
  698.9 42.9 %all-reduce.9.cloned.1.call-done = (bf16[256,1024]{1,0:T(8,128)(2,1)}, bf16[256,512]{1,0:T(8,128)(2,1)}, bf16[256,512]{1,0:T(8,128)(2,1)}, bf16[256,1024]{1,0:T(8,128)(2,1)}) async-done(((bf16[256,1024]{1,0:T(8,128)(2,1)}, bf16[256,512]{1,0:T(8,128)(2,1)}, bf16[256,512]{1,0:T(8,128)(2,1)}, bf16[256,1024]{1,0:T(8,128)(2,1)}), (bf16[256,1024]{1,0:T(8,128)(2,1)}, bf16[256,512]{1,0:T(8,128)(2,1)}, ...) | async-done | bytes 1572880 | tf_op jit(solution)/shard_map/psum | solution.py:349
  (283 shorter events, 95.3 us)
Async XLA Ops:
  7.2 232.2 %copy-start = (bf16[1,512,1024]{2,1,0:T(8,128)(2,1)S(1)}, bf16[1,512,1024]{2,1,0:T(8,128)(2,1)}, u32[]{:S(2)}) copy-start(bf16[1,512,1024]{2,1,0:T(8,128)(2,1)} %param.29) | copy-start | bytes 3145732
  7.2 14.0 %copy-start.71 = (s32[1,2]{1,0:T(1,128)S(1)}, s32[1,2]{1,0:T(1,128)}, u32[]{:S(2)}) copy-start(s32[1,2]{1,0:T(1,128)} %param.17) | copy-start | bytes 28
  7.2 14.2 %copy-start.72 = (bf16[256]{0:T(256)(128)(2,1)S(1)}, bf16[256]{0:T(256)(128)(2,1)}, u32[]{:S(2)}) copy-start(bf16[256]{0:T(256)(128)(2,1)} %param.20) | copy-start | bytes 1540
  7.2 14.2 %copy-start.73 = (bf16[256]{0:T(256)(128)(2,1)S(1)}, bf16[256]{0:T(256)(128)(2,1)}, u32[]{:S(2)}) copy-start(bf16[256]{0:T(256)(128)(2,1)} %param.25) | copy-start | bytes 1540
  7.2 15.3 %copy-start.7 = (bf16[512,1024]{1,0:T(8,128)(2,1)S(1)}, bf16[512,1024]{1,0:T(8,128)(2,1)}, u32[]{:S(2)}) copy-start(bf16[512,1024]{1,0:T(8,128)(2,1)} %param.16) | copy-start | bytes 3145732
  7.2 37.9 %all-gather.9.cloned.1.call-start = ((), (), s32[]{:S(2)}) async-start(), calls=%async_computation.13 | async-start | bytes 1310720 | tf_op jit(solution)/shard_map/all_gather | solution.py:88
  8.0 61.5 %all-gather.7.cloned.1.call-start = ((), (), s32[]{:S(2)}) async-start(), calls=%async_computation.12 | async-start | bytes 1310720 | tf_op jit(solution)/shard_map/all_gather | solution.py:89
  8.7 107.8 %all-gather.11.cloned.1.call-start = ((), (), s32[]{:S(2)}) async-start(), calls=%async_computation.14 | async-start | bytes 2621440 | tf_op jit(solution)/shard_map/all_gather | solution.py:87
  9.5 153.2 %all-gather.13.cloned.1.call-start = ((), (), s32[]{:S(2)}) async-start(), calls=%async_computation.15 | async-start | bytes 2621440 | tf_op jit(solution)/shard_map/all_gather | solution.py:90
  11.6 260.0 %copy-start.18 = (s32[512,2]{1,0:T(8,128)}, s32[512,2]{1,0:T(8,128)S(1)}, u32[]{:S(2)}) copy-start(s32[512,2]{1,0:T(8,128)S(1)} %copy.61) | copy-start | bytes 12292
  11.7 33.4 %copy-start.51 = (s32[1024]{0:T(1024)}, s32[1024]{0:T(1024)S(1)}, u32[]{:S(2)}) copy-start(s32[1024]{0:T(1024)S(1)} %eq.73) | copy-start | bytes 12292
  22.8 93.7 %copy-start.61 = (f32[512]{0:T(512)}, f32[512]{0:T(512)S(1)}, u32[]{:S(2)}) copy-start(f32[512]{0:T(512)S(1)} %add_rsqrt_fusion.1) | copy-start | bytes 6148
  44.2 72.3 %copy-start.55 = (f32[4,1,256]{2,1,0:T(1,128)}, f32[4,1,256]{2,1,0:T(1,128)S(1)}, u32[]{:S(2)}) copy-start(f32[4,1,256]{2,1,0:T(1,128)S(1)} %convert_element_type.260) | copy-start | bytes 12292
  45.1 74.4 %copy-start.27 = (f32[512,32]{0,1:T(8,128)}, f32[512,32]{0,1:T(8,128)S(1)}, u32[]{:S(2)}) copy-start(f32[512,32]{0,1:T(8,128)S(1)} %get-tuple-element.44) | copy-start | bytes 196612
  45.2 74.4 %copy-start.29 = (f32[512,32]{0,1:T(8,128)}, f32[512,32]{0,1:T(8,128)S(1)}, u32[]{:S(2)}) copy-start(f32[512,32]{0,1:T(8,128)S(1)} %get-tuple-element.45) | copy-start | bytes 196612
  119.9 8.2 %copy-start.20 = (bf16[512,16,32]{0,2,1:T(8,128)(2,1)}, bf16[512,16,32]{0,2,1:T(8,128)(2,1)S(1)}, u32[]{:S(2)}) copy-start(bf16[512,16,32]{0,2,1:T(8,128)(2,1)S(1)} %get-tuple-element.32) | copy-start | bytes 1572868
  119.9 8.2 %copy-start.22 = (bf16[512,16,32]{0,2,1:T(8,128)(2,1)}, bf16[512,16,32]{0,2,1:T(8,128)(2,1)S(1)}, u32[]{:S(2)}) copy-start(bf16[512,16,32]{0,2,1:T(8,128)(2,1)S(1)} %get-tuple-element.33) | copy-start | bytes 1572868
  128.1 8.3 %copy-start.43 = (bf16[512,512]{0,1:T(8,128)(2,1)S(1)}, bf16[512,512]{0,1:T(8,128)(2,1)}, u32[]{:S(2)}) copy-start(bf16[512,512]{0,1:T(8,128)(2,1)} %convolution_convert_fusion.9) | copy-start | bytes 1572868
  144.1 21.5 %copy-start.40 = (bf16[8,64,2,512]{3,1,2,0:T(8,128)(2,1)}, bf16[8,64,2,512]{3,1,2,0:T(8,128)(2,1)S(1)}, u32[]{:S(2)}) copy-start(bf16[8,64,2,512]{3,1,2,0:T(8,128)(2,1)S(1)} %fusion.24) | copy-start | bytes 3145732
  165.9 105.3 %copy-start.5 = (bf16[512,1024]{1,0:T(8,128)(2,1)}, bf16[512,1024]{1,0:T(8,128)(2,1)S(1)}, u32[]{:S(2)}) copy-start(bf16[512,1024]{1,0:T(8,128)(2,1)S(1)} %multiply_convert_fusion.4) | copy-start | bytes 3145732
  166.9 9.7 %copy-start.64 = (pred[8,256]{1,0:T(8,128)(4,1)S(1)}, pred[8,256]{1,0:T(8,128)(4,1)}, u32[]{:S(2)}) copy-start(pred[8,256]{1,0:T(8,128)(4,1)} %broadcast_in_dim.67) | copy-start | bytes 6148
  179.1 52.8 %copy-start.67 = (bf16[1,1024,512]{2,1,0:T(8,128)(2,1)S(1)}, bf16[1,1024,512]{2,1,0:T(8,128)(2,1)}, u32[]{:S(2)}) copy-start(bf16[1,1024,512]{2,1,0:T(8,128)(2,1)} %param.27) | copy-start | bytes 3145732
  243.8 53.8 %all-to-all-start.1 = ((bf16[8,256,1024]{2,1,0:T(8,128)(2,1)}), bf16[8,256,1024]{2,1,0:T(8,128)(2,1)}, u32[]{:S(2)}, u32[]{:S(2)}) async-start(bf16[8,256,1024]{2,1,0:T(8,128)(2,1)} %bitcast.196), calls=%async_computation.1 | async-start | bytes 8388608 | tf_op jit(solution)/shard_map/all_to_all | solution.py:182
  248.5 303.3 %reduce-scatter.23.cloned.1.call-start = ((), (), s32[]{:S(2)}) async-start(), calls=%async_computation.23 | async-start | bytes 1310720 | tf_op jit(solution)/shard_map/reduce_scatter | solution.py:344
  251.7 19.4 %copy-start.52 = (s32[1024]{0:T(1024)S(1)}, s32[1024]{0:T(1024)}, u32[]{:S(2)}) copy-start(s32[1024]{0:T(1024)} %copy-done.51) | copy-start | bytes 12292
  251.7 19.4 %copy-start.54 = (s32[1024]{0:T(1024)S(1)}, s32[1024]{0:T(1024)}, u32[]{:S(2)}) copy-start(s32[1024]{0:T(1024)} %copy-done.53) | copy-start | bytes 12292
  273.3 24.3 %copy-start.16 = (f32[512,1,2]{2,1,0:T(1,128)}, f32[512,1,2]{2,1,0:T(1,128)S(1)}, u32[]{:S(2)}) copy-start(f32[512,1,2]{2,1,0:T(1,128)S(1)} %fusion.50) | copy-start | bytes 12292
  333.1 54.1 %copy-start.79 = (bf16[2048,512]{1,0:T(8,128)(2,1)S(1)}, bf16[2048,512]{1,0:T(8,128)(2,1)}, u32[]{:S(2)}) copy-start(bf16[2048,512]{1,0:T(8,128)(2,1)} %copy-done.78) | copy-start | bytes 6291460
  390.6 8.7 %copy-start.68 = (bf16[1,1024,512]{2,1,0:T(8,128)(2,1)S(1)}, bf16[1,1024,512]{2,1,0:T(8,128)(2,1)}, u32[]{:S(2)}) copy-start(bf16[1,1024,512]{2,1,0:T(8,128)(2,1)} %param.27) | copy-start | bytes 3145732
  408.1 53.8 %all-to-all-start.3 = ((bf16[8,256,1024]{2,1,0:T(8,128)(2,1)}), bf16[8,256,1024]{2,1,0:T(8,128)(2,1)}, u32[]{:S(2)}, u32[]{:S(2)}) async-start(bf16[8,256,1024]{2,1,0:T(8,128)(2,1)} %bitcast.195), calls=%async_computation.3 | async-start | bytes 8388608 | tf_op jit(solution)/shard_map/all_to_all | solution.py:227
  412.8 140.7 %reduce-scatter.21.cloned.1.call-start = ((), (), s32[]{:S(2)}) async-start(), calls=%async_computation.22 | async-start | bytes 1310720 | tf_op jit(solution)/shard_map/reduce_scatter | solution.py:341
  418.5 136.9 %reduce-scatter.19.cloned.1.call-start = ((), (), s32[]{:S(2)}) async-start(), calls=%async_computation.21 | async-start | bytes 1310720 | tf_op jit(solution)/shard_map/reduce_scatter | solution.py:338
  429.0 135.0 %reduce-scatter.13.cloned.1.call-start = ((), (), s32[]{:S(2)}) async-start(), calls=%async_computation.18 | async-start | bytes 1310720 | tf_op jit(solution)/shard_map/reduce_scatter | solution.py:326
  477.9 8.7 %copy-start.4 = (f32[512,1024]{1,0:T(8,128)S(1)}, f32[512,1024]{1,0:T(8,128)}, u32[]{:S(2)}) copy-start(f32[512,1024]{1,0:T(8,128)} %copy-done.3) | copy-start | bytes 6291460
  477.9 8.7 %copy-start.39 = (f32[512,1,8]{2,1,0:T(1,128)S(1)}, f32[512,1,8]{2,1,0:T(1,128)}, u32[]{:S(2)}) copy-start(f32[512,1,8]{2,1,0:T(1,128)} %fusion.49) | copy-start | bytes 49156
  477.9 8.7 %copy-start.50 = (f32[4,1,256]{2,1,0:T(1,128)S(1)}, f32[4,1,256]{2,1,0:T(1,128)}, u32[]{:S(2)}) copy-start(f32[4,1,256]{2,1,0:T(1,128)} %convert_element_type.261) | copy-start | bytes 12292
  477.9 8.7 %copy-start.60 = (f32[512]{0:T(512)S(1)}, f32[512]{0:T(512)}, u32[]{:S(2)}) copy-start(f32[512]{0:T(512)} %copy-done.59) | copy-start | bytes 6148
  495.0 8.6 %copy-start.8 = (bf16[512,1024]{1,0:T(8,128)(2,1)S(1)}, bf16[512,1024]{1,0:T(8,128)(2,1)}, u32[]{:S(2)}) copy-start(bf16[512,1024]{1,0:T(8,128)(2,1)} %param.16) | copy-start | bytes 3145732
  495.0 8.6 %copy-start.56 = (f32[4,1,256]{2,1,0:T(1,128)S(1)}, f32[4,1,256]{2,1,0:T(1,128)}, u32[]{:S(2)}) copy-start(f32[4,1,256]{2,1,0:T(1,128)} %copy-done.55) | copy-start | bytes 12292
  495.0 8.6 %copy-start.62 = (f32[512]{0:T(512)S(1)}, f32[512]{0:T(512)}, u32[]{:S(2)}) copy-start(f32[512]{0:T(512)} %copy-done.61) | copy-start | bytes 6148
  516.3 53.1 %reduce-scatter.11.cloned.1.call-start = ((), (), s32[]{:S(2)}) async-start(), calls=%async_computation.17 | async-start | bytes 1310720 | tf_op jit(solution)/shard_map/reduce_scatter | solution.py:323
  516.4 12.6 %copy-start.21 = (bf16[512,16,32]{0,2,1:T(8,128)(2,1)S(1)}, bf16[512,16,32]{0,2,1:T(8,128)(2,1)}, u32[]{:S(2)}) copy-start(bf16[512,16,32]{0,2,1:T(8,128)(2,1)} %copy-done.20) | copy-start | bytes 1572868
  516.4 12.6 %copy-start.23 = (bf16[512,16,32]{0,2,1:T(8,128)(2,1)S(1)}, bf16[512,16,32]{0,2,1:T(8,128)(2,1)}, u32[]{:S(2)}) copy-start(bf16[512,16,32]{0,2,1:T(8,128)(2,1)} %copy-done.22) | copy-start | bytes 1572868
  534.4 79.8 %reduce-scatter.15.cloned.1.call-start = ((), (), s32[]{:S(2)}) async-start(), calls=%async_computation.19 | async-start | bytes 2621440 | tf_op jit(solution)/shard_map/reduce_scatter | solution.py:329
  538.7 121.0 %reduce-scatter.9.cloned.1.call-start = ((), (), s32[]{:S(2)}) async-start(), calls=%async_computation.16 | async-start | bytes 2621440 | tf_op jit(solution)/shard_map/reduce_scatter | solution.py:320
  548.9 131.9 %reduce-scatter.17.cloned.1.call-start = ((), (), s32[]{:S(2)}) async-start(), calls=%async_computation.20 | async-start | bytes 20480 | tf_op jit(solution)/shard_map/reduce_scatter | solution.py:335
  551.7 190.1 %all-reduce.9.cloned.1.call-start = ((), (), s32[]{:S(2)}) async-start(), calls=%async_computation.24 | async-start | bytes 3145728 | tf_op jit(solution)/shard_map/psum | solution.py:349
  564.0 95.8 %copy-start.42 = (bf16[1024,512]{1,0:T(8,128)(2,1)S(1)}, bf16[1024,512]{1,0:T(8,128)(2,1)}, u32[]{:S(2)}) copy-start(bf16[1024,512]{1,0:T(8,128)(2,1)} %all-gather.7.cloned.1.call-done) | copy-start | bytes 3145732
  (48 other events, 145.5 us)
Sparse Core Ops, SparseCore 0:
  9.6 30.7 all-gather.8
  42.0 27.4 all-gather.6
  71.0 45.4 all-gather.10
  117.9 44.6 all-gather.12
  399.4 24.0 reduce-scatter.22
  425.7 25.7 reduce-scatter.20
  453.8 25.7 reduce-scatter.18
  516.4 24.2 reduce-scatter.12
  543.6 25.7 reduce-scatter.10
  571.7 42.5 reduce-scatter.14
  616.5 43.1 reduce-scatter.8
  662.5 18.2 reduce-scatter.16
  684.3 57.4 all-reduce.8
where the time goes:
time: 759 us; the launch traced here: 755 us
  waiting for transfers between devices  289 us (38%)
  blocking collectives  161 us (21%)
  matrix products  136 us (18%)
  local copies, waits for them, and re-layouts  71.9 us (9%)
  other arithmetic  70.7 us (9%)
  between operations  16 us (2%)
  starting transfers between devices  10.3 us (1%)
    all_to_all x1, blocking collectives, local(): lax.all_to_all(outgoing, 'expert', split_axis=0, concat_axis=0, tiled=True)  52.8 us
    all_to_all x1, blocking collectives, local(): lax.all_to_all(outgoing_grad, 'expert', split_axis=0, concat_axis=0, tile...  52.1 us
    reduce_scatter x1, waiting for transfers between devices, local(): lax.psum_scatter(grad_query_w.astype(jnp.bfloat16), 'dp', scatter_dimensi...  45.5 us
    reduce_scatter x1, waiting for transfers between devices, local(): lax.psum_scatter(grad_out_w.astype(jnp.bfloat16), 'dp', scatter_dimension...  44.8 us
    all_gather x1, waiting for transfers between devices, local(): lax.all_gather(w_query, 'dp', axis=0, tiled=True)  44.2 us
    psum x1, waiting for transfers between devices, local(): lax.psum(as_sent(tuple(local_parts[:7])), 'expert')  42.9 us
    all_to_all x1, waiting for transfers between devices, local(): lax.all_to_all(grad_send, 'expert', split_axis=0, concat_axis=0, tiled=True)  32.9 us
    all_to_all x1, waiting for transfers between devices, local(): lax.all_to_all(result, 'expert', split_axis=0, concat_axis=0, tiled=True)  23.9 us
  transfers between devices with their start and end apart: 15, of which 10 were waited for; matrix products, arithmetic and copies ran while one was open for 25% of the time, Pallas kernels for 0%

commit v1 on v0

v1 whole, which is shorter than its diff:
```python
import math

import jax
import jax.numpy as jnp
from jax import lax
from jax.experimental import pallas as pl
from jax.experimental.pallas import tpu as pltpu
from jax.sharding import PartitionSpec as P

QUERY_HEADS = 16
KEY_VALUE_HEADS = 8
HEAD_DIMENSION = 64


eps_norm = 1e-06


def positions_of(lengths_row, count_of_rows):
    index_rows = jnp.arange(count_of_rows, dtype=jnp.int32)
    ends = jnp.cumsum(lengths_row)
    member = jnp.sum((index_rows[:, None] >= ends[None, :]).astype(jnp.int32), axis=1)
    starts = ends - lengths_row
    onehot = member[:, None] == jnp.arange(lengths_row.shape[0], dtype=jnp.int32)[None, :]
    begin = jnp.sum(jnp.where(onehot, starts[None, :], 0), axis=1)
    return (member, index_rows - begin)


def rope_tables(positions, head_size):
    half_size = head_size // 2
    freq = jnp.exp(
        jnp.arange(half_size, dtype=jnp.float32) * (-2.0 * math.log(10000.0) / head_size)
    )
    angle = positions.astype(jnp.float32)[:, None] * freq[None, :]
    return (jnp.cos(angle), jnp.sin(angle))


def apply_rotary(values, cosine_table, sine_table):
    half_size = values.shape[-1] // 2
    first = values[..., :half_size]
    second = values[..., half_size:]
    cos_b = cosine_table[:, None, :]
    sin_b = sine_table[:, None, :]
    return jnp.concatenate(
        [first * cos_b - second * sin_b, second * cos_b + first * sin_b], axis=-1
    )


def reverse_rotary(grads, cosine_table, sine_table):
    half_size = grads.shape[-1] // 2
    first = grads[..., :half_size]
    second = grads[..., half_size:]
    cos_b = cosine_table[:, None, :]
    sin_b = sine_table[:, None, :]
    return jnp.concatenate(
        [first * cos_b + second * sin_b, second * cos_b - first * sin_b], axis=-1
    )


F32 = jnp.float32
BF16 = jnp.bfloat16
VMEM_LIMIT = 56 * 1024 * 1024


def hop(values, axis, mask):
    count = lax.axis_size(axis)
    return lax.ppermute(values, axis, [(i, i ^ mask) for i in range(count)])


def link_bits(count):
    return [1 << i for i in range(1, count.bit_length() - 1)]


def after(values, *earlier):
    return lax.optimization_barrier((values, *earlier))[0]


def spread_half(piece, count, order):
    blocks = {0: piece}
    for bit in order:
        for m in list(blocks):
            blocks[m ^ bit] = hop(blocks[m], "expert", bit)
    for m in list(blocks):
        blocks[m ^ 1] = hop(blocks[m], "expert", 1)
    return blocks


def gather_plane(first, second):
    count = lax.axis_size("expert")
    bits = link_bits(count)
    return spread_half(first, count, bits), spread_half(second, count, bits[::-1])


def gather_small(values):
    count = lax.axis_size("expert")
    rows = values[None]
    bit = 1
    while bit < count:
        rows = jnp.concatenate([rows, hop(rows, "expert", bit)], axis=0)
        bit *= 2
    return rows


def place_kernel(devices, count, rows, *refs):
    pieces, own_ref, out_ref, sems = refs[:-3], refs[-3], refs[-2], refs[-1]
    z_index = lax.axis_index("dp")
    e_index = lax.axis_index("expert")
    shard_rows = own_ref.shape[0]
    width = out_ref.shape[1]
    half = width // 2
    copies = [
        pltpu.make_async_copy(
            own_ref,
            out_ref.at[pl.ds(pl.multiple_of(z_index * shard_rows, 16), shard_rows), :],
            sems.at[0],
        )
    ]
    for side in range(2):
        for m in range(count):
            piece = pieces[side * count + m]
            for zm in range(1, devices):
                start = (z_index ^ zm) * shard_rows + (e_index ^ m) * rows
                copies.append(
                    pltpu.make_async_copy(
                        piece.at[pl.ds((zm - 1) * rows, rows), :],
                        out_ref.at[
                            pl.ds(pl.multiple_of(start, 16), rows), pl.ds(side * half, half)
                        ],
                        sems.at[len(copies)],
                    )
                )
    for copy in copies:
        copy.start()
    for copy in copies:
        copy.wait()


def gather_weight(shard):
    devices = lax.axis_size("dp")
    count = lax.axis_size("expert")
    shard_rows, width = shard.shape
    rows = shard_rows // count
    if rows % 16 or width % 256:
        return lax.all_gather(shard, "dp", axis=0, tiled=True)
    mine = lax.dynamic_slice_in_dim(shard, lax.axis_index("expert") * rows, rows, 0)
    far = jnp.concatenate([hop(mine, "dp", m) for m in range(1, devices)], axis=0)
    one, two = gather_plane(far[:, : width // 2], far[:, width // 2 :])
    pieces = [one[m] for m in range(count)] + [two[m] for m in range(count)]
    any_space = pl.BlockSpec(memory_space=pl.ANY)
    return pl.pallas_call(
        lambda *refs: place_kernel(devices, count, rows, *refs),
        out_shape=jax.ShapeDtypeStruct((shard_rows * devices, width), shard.dtype),
        in_specs=[any_space] * (len(pieces) + 1),
        out_specs=any_space,
        scratch_shapes=[pltpu.SemaphoreType.DMA((1 + 2 * count * (devices - 1),))],
        name="place_weight",
    )(*pieces, shard)


def bit_of(index, bit):
    return (index // bit) % 2


def reduce_weight(total):
    devices = lax.axis_size("dp")
    count = lax.axis_size("expert")
    height, width = total.shape
    rows = height // (devices * count)
    if rows % 16:
        part = lax.psum_scatter(total, "dp", scatter_dimension=0, tiled=True)
        return lax.psum(part, "expert").astype(F32)
    z_index = lax.axis_index("dp")
    e_index = lax.axis_index("expert")
    bits = [1 << i for i in range(count.bit_length() - 1)]
    levels = len(bits)

    def axis_of(bit):
        return levels - bit.bit_length() + 1

    def split(part, bit):
        mine = bit_of(e_index, bit)
        axis = axis_of(bit)
        send = lax.dynamic_index_in_dim(part, 1 - mine, axis, keepdims=True)
        keep = lax.dynamic_index_in_dim(part, mine, axis, keepdims=True)
        return (keep.astype(F32) + hop(send, "expert", bit).astype(F32)).astype(BF16)

    whole = total.reshape((devices,) + (2,) * levels + (rows, width))
    near = split(whole, 1)
    halves = [near[: devices // 2], near[devices // 2 :]]
    for side, order in enumerate((bits[1:], bits[1:][::-1])):
        for bit in order:
            halves[side] = split(halves[side], bit)
    line = jnp.concatenate(halves, axis=0).reshape(devices, rows, width)
    done = lax.dynamic_index_in_dim(line, z_index, 0, keepdims=False).astype(F32)
    for m in range(1, devices):
        piece = lax.dynamic_index_in_dim(line, z_index ^ m, 0, keepdims=False)
        done = done + hop(piece, "dp", m).astype(F32)
    done = done.astype(BF16)

    def join(part, bit):
        other = hop(part, "expert", bit)
        axis = axis_of(bit) - 1
        return jnp.where(
            bit_of(e_index, bit) == 0,
            jnp.concatenate([part, other], axis=axis),
            jnp.concatenate([other, part], axis=axis),
        )

    done = join(done.reshape((1,) * levels + (rows, width)), 1)
    sides = [done[..., : width // 2], done[..., width // 2 :]]
    for side, order in enumerate((bits[1:], bits[1:][::-1])):
        for bit in order:
            sides[side] = join(sides[side], bit)
    return jnp.concatenate(sides, axis=-1).reshape(count * rows, width).astype(F32)


def reduce_small(values):
    for axis in ("expert", "dp"):
        bit = 1
        while bit < lax.axis_size(axis):
            values = values + hop(values, axis, bit)
            bit *= 2
    return values


def scatter_line(pieces):
    devices = lax.axis_size("dp")
    z_index = lax.axis_index("dp")

    def at(index):
        return lax.dynamic_index_in_dim(pieces, index % devices, 0, keepdims=False)

    right = left = None
    for step in range(1, devices):
        give_right = at(z_index + devices - step)
        give_left = at(z_index + step)
        if right is not None:
            give_right = (give_right.astype(F32) + right.astype(F32)).astype(BF16)
            give_left = (give_left.astype(F32) + left.astype(F32)).astype(BF16)
        right = lax.ppermute(give_right, "dp", [(i, i + 1) for i in range(step) if i + 1 < devices])
        left = lax.ppermute(
            give_left, "dp", [(devices - 1 - i, devices - 2 - i) for i in range(step)]
        )
    return at(z_index).astype(F32) + right.astype(F32) + left.astype(F32)


def pick_rows(slots, capacity):
    index = lax.broadcasted_iota(jnp.int32, (capacity, slots.shape[1]), 0)
    return index == slots


def expert_kernel(capacity, *refs):
    tok, cot = refs[0:4], refs[4:8]
    slot_ref, route_ref, mine_ref, router_ref, gate_up_ref, down_ref = refs[8:14]
    (keep_moe, give_moe, keep_in, give_in, rows_ref, ge_ref, hid_ref, dgu_ref, gg_ref) = refs[14:23]
    drows_ref, chosen_ref, gg_col = refs[23:]
    half = tok[0].shape[0]
    lanes = mine_ref.shape[1]
    top = route_ref.shape[1]
    hidden_width = hid_ref.shape[1]
    for b in range(2):
        sel = pick_rows(slot_ref[b : b + 1, :], capacity).astype(F32).astype(BF16)
        place = pl.ds(b * capacity, capacity)
        for source, target in ((tok, rows_ref), (cot, drows_ref)):
            target[place, :] = (
                jnp.dot(sel[:, :half], source[2 * b][...], preferred_element_type=F32)
                + jnp.dot(sel[:, half:], source[2 * b + 1][...], preferred_element_type=F32)
            ).astype(BF16)
        expert = lax.broadcasted_iota(jnp.int32, (lanes, 2 * half), 0)
        named = route_ref[b, 0:1, :] == expert
        for k in range(1, top):
            named = named | (route_ref[b, k : k + 1, :] == expert)
        chosen_ref[place, :] = lax.dot_general(
            sel,
            named.astype(F32).astype(BF16),
            (((1,), (1,)), ((), ())),
            preferred_element_type=F32,
        )

    for b in range(2):
        place = pl.ds(b * capacity, capacity)
        rows = rows_ref[place, :]
        drows = drows_ref[place, :].astype(F32)
        logits = jnp.dot(rows, router_ref[...], preferred_element_type=F32)
        chosen = chosen_ref[place, :] > 0.5
        shown = jnp.where(chosen, logits, -1e30)
        weight = jnp.where(chosen, jnp.exp(shown - jnp.max(shown, axis=-1, keepdims=True)), 0.0)
        total = jnp.sum(weight, axis=-1, keepdims=True)
        gate = jnp.sum(weight * mine_ref[...], axis=-1, keepdims=True) / jnp.where(
            total > 0.0, total, 1.0
        )
        gate_up = jnp.dot(rows, gate_up_ref[...], preferred_element_type=F32)
        gate_pre = gate_up[:, :hidden_width]
        up_pre = gate_up[:, hidden_width:]
        sigm = 1.0 / (1.0 + jnp.exp(-gate_pre))
        activated = gate_pre * sigm
        hidden = (activated * up_pre).astype(BF16)
        hid_ref[place, :] = hidden
        result = jnp.dot(hidden, down_ref[...], preferred_element_type=F32)
        result = result.astype(BF16).astype(F32)
        gg_col[place, :] = jnp.sum(drows * result, axis=-1, keepdims=True)
        moe = (give_moe if b else keep_moe)
        moe[...] = (gate * result).astype(BF16)
        grad_out = (gate * drows).astype(BF16)
        ge_ref[place, :] = grad_out
        grad_hidden = lax.dot_general(
            grad_out, down_ref[...], (((1,), (1,)), ((), ())), preferred_element_type=F32
        )
        dgate = (grad_hidden * up_pre * sigm * (1.0 + gate_pre * (1.0 - sigm))).astype(BF16)
        dup = (grad_hidden * activated).astype(BF16)
        dgu_ref[place, :hidden_width] = dgate
        dgu_ref[place, hidden_width:] = dup
        grad_in = lax.dot_general(
            dgu_ref[place, :], gate_up_ref[...], (((1,), (1,)), ((), ())), preferred_element_type=F32
        )
        back = (give_in if b else keep_in)
        back[...] = grad_in.astype(BF16)
        picked = pick_rows(slot_ref[b : b + 1, :], capacity)
        gg_ref[b : b + 1, :] = jnp.sum(
            jnp.where(picked, gg_col[place, :], 0.0), axis=0, keepdims=True
        )


def expert_group(tok, cot, slots, routes, mine, router, gate_up, down, capacity):
    width = tok[0].shape[1]
    hidden = down.shape[0]
    tokens = slots.shape[1]
    low = lambda *shape: jax.ShapeDtypeStruct(shape, BF16)
    rows = 2 * capacity
    vmem = pl.BlockSpec(memory_space=pltpu.VMEM)
    flops = 2 * rows * width * hidden * 6 + 4 * rows * tokens * width
    return pl.pallas_call(
        lambda *refs: expert_kernel(capacity, *refs),
        out_shape=(
            low(capacity, width),
            low(capacity, width),
            low(capacity, width),
            low(capacity, width),
            low(rows, width),
            low(rows, width),
            low(rows, hidden),
            low(rows, 2 * hidden),
            jax.ShapeDtypeStruct((2, tokens), F32),
        ),
        in_specs=[vmem] * 14,
        out_specs=[vmem] * 9,
        scratch_shapes=[
            pltpu.VMEM((rows, width), BF16),
            pltpu.VMEM((rows, mine.shape[1]), F32),
            pltpu.VMEM((rows, 1), F32),
        ],
        compiler_params=pltpu.CompilerParams(vmem_limit_bytes=VMEM_LIMIT),
        cost_estimate=pl.CostEstimate(
            flops=flops, bytes_accessed=16 * 1024 * 1024, transcendentals=rows * hidden
        ),
        name="expert_group",
    )(*tok, *cot, slots, routes, mine, router, gate_up, down)


def combine_kernel(capacity, keep_ref, sib_ref, slot_ref, *outs):
    half = outs[0].shape[0]
    for side, out in enumerate(outs):
        total = None
        for who, rows in enumerate((keep_ref, sib_ref)):
            sel = pick_rows(slot_ref[who : who + 1, side * half : (side + 1) * half], capacity)
            part = lax.dot_general(
                sel.astype(F32).astype(BF16),
                rows[...],
                (((0,), (0,)), ((), ())),
                preferred_element_type=F32,
            )
            total = part if total is None else total + part
        out[...] = total.astype(BF16)


def combine(keep, sib, slots):
    capacity, width = keep.shape
    tokens = slots.shape[1]
    vmem = pl.BlockSpec(memory_space=pltpu.VMEM)
    return pl.pallas_call(
        lambda *refs: combine_kernel(capacity, *refs),
        out_shape=(jax.ShapeDtypeStruct((tokens // 2, width), BF16),) * 2,
        in_specs=[vmem] * 3,
        out_specs=[vmem] * 2,
        compiler_params=pltpu.CompilerParams(vmem_limit_bytes=VMEM_LIMIT),
        cost_estimate=pl.CostEstimate(
            flops=4 * tokens * capacity * width, bytes_accessed=2 * 1024 * 1024, transcendentals=0
        ),
        name="combine_rows",
    )(keep, sib, slots)


def wgrad_kernel(groups, gate_rows, down_rows, *refs):
    rows, ge, hid, dgu = (refs[i * groups : (i + 1) * groups] for i in range(4))
    out = refs[4 * groups]
    for left, right, start, count in (
        (rows, dgu, 0, gate_rows),
        (hid, ge, gate_rows, down_rows),
    ):
        total = None
        for g in range(groups):
            part = lax.dot_general(
                left[g][...], right[g][...], (((0,), (0,)), ((), ())), preferred_element_type=F32
            )
            total = part if total is None else total + part
        out[0, start : start + count, :] = total.astype(BF16)


def expert_wgrad(rows, ge, hid, dgu):
    devices = lax.axis_size("dp")
    groups = len(rows)
    width = rows[0].shape[1]
    hidden = hid[0].shape[1]
    gate_rows, down_rows = width // devices, hidden // devices
    if groups > 4 or gate_rows % 128 or down_rows % 128:
        everything = [jnp.concatenate(part, axis=0) for part in (rows, ge, hid, dgu)]
        gate_up = jnp.dot(everything[0].T, everything[3], preferred_element_type=F32)
        down = jnp.dot(everything[2].T, everything[1], preferred_element_type=F32)
        return jnp.concatenate(
            [
                gate_up.astype(BF16).reshape(devices, gate_rows, 2 * hidden),
                down.astype(BF16).reshape(devices, down_rows, width),
            ],
            axis=1,
        )
    count = rows[0].shape[0]
    sliced = lambda size: pl.BlockSpec((count, size), lambda i: (0, i))
    fixed = lambda size: pl.BlockSpec((count, size), lambda i: (0, 0))
    return pl.pallas_call(
        lambda *refs: wgrad_kernel(groups, gate_rows, down_rows, *refs),
        grid=(devices,),
        out_shape=jax.ShapeDtypeStruct((devices, gate_rows + down_rows, width), BF16),
        in_specs=[sliced(gate_rows)] * groups
        + [fixed(width)] * groups
        + [sliced(down_rows)] * groups
        + [fixed(2 * hidden)] * groups,
        out_specs=pl.BlockSpec((1, gate_rows + down_rows, width), lambda i: (i, 0, 0)),
        compiler_params=pltpu.CompilerParams(vmem_limit_bytes=VMEM_LIMIT),
        cost_estimate=pl.CostEstimate(
            flops=2 * groups * count * width * hidden * 3,
            bytes_accessed=16 * 1024 * 1024,
            transcendentals=0,
        ),
        name="expert_wgrad",
    )(*rows, *ge, *hid, *dgu)


def return_plane(partial):
    count = lax.axis_size("expert")
    bits = link_bits(count)
    results = []
    for side, order in enumerate((bits, bits[::-1])):
        blocks = {m: partial[m][side] for m in partial}
        for bit in order:
            arrived = {
                m: hop(blocks[m], "expert", bit) for m in sorted(blocks, reverse=True) if m & bit
            }
            blocks = {m: blocks[m] for m in blocks if not m & bit}
            if bit == order[-1]:
                results.append((blocks[0], arrived[bit]))
            else:
                blocks = {
                    m: (blocks[m].astype(F32) + arrived[m | bit].astype(F32)).astype(BF16)
                    for m in blocks
                }
    return results


def join_halves(results):
    return jnp.concatenate([a.astype(F32) + b.astype(F32) for a, b in results], axis=0)


def local(
    tokens,
    lengths,
    routes,
    cotangent,
    gain_attn,
    w_query,
    key_projection_weight,
    value_projection_weight,
    w_out,
    gain_moe,
    w_router,
    w_gate,
    w_up,
    w_down,
):
    single_float = F32
    brain_float_half = BF16
    count_of_rows, model_width = tokens.shape
    half_rows = count_of_rows // 2
    expert_count = lax.axis_size("expert")
    devices = lax.axis_size("dp")
    e_index = lax.axis_index("expert")
    z_index = lax.axis_index("dp")
    top_count = routes.shape[1]
    capacity = 2 * count_of_rows * top_count // expert_count
    group_factor = QUERY_HEADS // KEY_VALUE_HEADS
    scale = HEAD_DIMENSION ** (-0.5)
    shard_rows = gain_attn.shape[0]

    small = jnp.concatenate([gain_attn[None], gain_moe[None], w_router.T], axis=0)
    pad = -small.shape[0] % 16
    small = jnp.pad(small, ((0, pad), (0, 0)))
    small_all = jnp.stack([small] + [hop(small, "dp", m) for m in range(1, devices)])
    small_all = jnp.take(small_all, z_index ^ jnp.arange(devices), axis=0)
    small_all = small_all.transpose(1, 0, 2).reshape(small.shape[0], model_width)
    gain_first = small_all[0].astype(F32)
    gain_second = small_all[1].astype(F32)
    router_w = small_all[2 : 2 + expert_count].T
    lanes = -(-expert_count // 128) * 128
    router_wide = jnp.pad(router_w, ((0, 0), (0, lanes - expert_count)))

    qkv_w = gather_weight(
        jnp.concatenate([w_query, key_projection_weight, value_projection_weight], axis=1)
    )
    out_w = gather_weight(w_out)
    query_width = w_query.shape[1]
    key_width = key_projection_weight.shape[1]

    routes_rel = gather_small(routes.T)
    before = (
        jnp.arange(count_of_rows)[:, None] < jnp.arange(count_of_rows)[None, :]
    ).astype(BF16)

    def slots_of(expert):
        hit = jnp.any(routes_rel == expert, axis=1)
        place = jnp.dot(hit.astype(BF16), before, preferred_element_type=F32)
        return jnp.where(hit, place.astype(jnp.int32), -1)

    slots_mine = slots_of(e_index)
    slots_sibling = slots_of(e_index ^ 1)
    mine_row = (jnp.arange(lanes) == e_index).astype(F32)[None]
    gate_up_w = jnp.concatenate([w_gate[0], w_up[0]], axis=1)
    down_w = w_down[0]

    resid_in = tokens.astype(single_float)
    inverse_one = lax.rsqrt(jnp.mean(resid_in * resid_in, axis=-1, keepdims=True) + eps_norm)
    first_normalized = (resid_in * inverse_one * gain_first).astype(brain_float_half)
    qkv = jnp.dot(first_normalized, qkv_w, preferred_element_type=single_float)
    query_before_rotation = qkv[:, :query_width].reshape(
        count_of_rows, QUERY_HEADS, HEAD_DIMENSION
    )
    key_before_rotation = qkv[:, query_width : query_width + key_width].reshape(
        count_of_rows, KEY_VALUE_HEADS, HEAD_DIMENSION
    )
    value_before_mixing = qkv[:, query_width + key_width :]
    cot_one, cot_two = gather_plane(
        after(cotangent[:half_rows], qkv_w), after(cotangent[half_rows:], qkv_w)
    )
    member, position = positions_of(lengths[0], count_of_rows)
    cosine_table, sine_table = rope_tables(position, HEAD_DIMENSION)
    query_vectors = (
        apply_rotary(query_before_rotation, cosine_table, sine_table)
        .astype(brain_float_half)
        .reshape(count_of_rows, KEY_VALUE_HEADS, group_factor, HEAD_DIMENSION)
    )
    key_row_block = apply_rotary(key_before_rotation, cosine_table, sine_table).astype(
        brain_float_half
    )
    value_row_block = value_before_mixing.astype(brain_float_half).reshape(
        count_of_rows, KEY_VALUE_HEADS, HEAD_DIMENSION
    )
    index_rows = jnp.arange(count_of_rows, dtype=jnp.int32)
    allowed = (member[:, None] == member[None, :]) & (index_rows[:, None] >= index_rows[None, :])

    def masked_scores():
        raw_scores = (
            jnp.einsum(
                "qcgd,kcd->cgqk", query_vectors, key_row_block, preferred_element_type=single_float
            )
            * scale
        )
        return jnp.where(allowed, raw_scores, -1e30)

    scores = masked_scores()
    row_peak = jnp.max(scores, axis=-1, keepdims=True)
    shifted_exp = jnp.exp(scores - row_peak)
    row_total = jnp.sum(shifted_exp, axis=-1, keepdims=True)
    probs = (shifted_exp / row_total).astype(brain_float_half)
    log_total = row_peak + jnp.log(row_total)
    mixed_heads = jnp.einsum(
        "cgqk,kcd->qcgd", probs, value_row_block, preferred_element_type=single_float
    )
    attn_rows = mixed_heads.reshape(count_of_rows, QUERY_HEADS * HEAD_DIMENSION).astype(
        brain_float_half
    )
    resid_mid = resid_in + jnp.dot(attn_rows, out_w, preferred_element_type=single_float)
    inverse_two = lax.rsqrt(jnp.mean(resid_mid * resid_mid, axis=-1, keepdims=True) + eps_norm)
    normed_two = (resid_mid * inverse_two * gain_second).astype(brain_float_half)

    tok_one, tok_two = gather_plane(normed_two[:half_rows], normed_two[half_rows:])

    logits = jnp.dot(normed_two, router_w, preferred_element_type=single_float)
    expert_ids = jnp.arange(expert_count, dtype=jnp.int32)
    chosen = (routes[:, :, None] == expert_ids[None, None, :]).astype(single_float)
    picked = jnp.sum(logits[:, None, :] * chosen, axis=-1)
    gates = jax.nn.softmax(picked, axis=-1)

    moe_partial, in_partial, saved, gg_rows = {}, {}, [], {}
    pending = {}
    for low_mask in range(0, expert_count, 2):
        pair = (low_mask, low_mask ^ 1)
        tok = [side[m] for m in pair for side in (tok_one, tok_two)]
        cot = [side[m] for m in pair for side in (cot_one, cot_two)]
        keep_moe, give_moe, keep_in, give_in, rows, ge, hid, dgu, gg = expert_group(
            tok,
            cot,
            slots_mine[low_mask : low_mask + 2],
            routes_rel[low_mask : low_mask + 2],
            mine_row,
            router_wide,
            gate_up_w,
            down_w,
            capacity,
        )
        saved.append((rows, ge, hid, dgu))
        slots = jnp.stack([slots_mine[low_mask], slots_sibling[low_mask]])
        in_partial[low_mask] = combine(keep_in, hop(give_in, "expert", 1), slots)
        pending[low_mask] = (keep_moe, give_moe, slots)
        gg_rows[low_mask] = gg[0]
        gg_rows[low_mask ^ 1] = gg[1]

    grad_result = return_plane(in_partial)
    gg_all = jnp.stack(
        [gg_rows[0]] + [hop(gg_rows[m], "expert", m) for m in range(1, expert_count)]
    )
    for low_mask, (keep_moe, give_moe, slots) in pending.items():
        give_moe = after(give_moe, *[r[1] for r in grad_result])
        moe_partial[low_mask] = combine(keep_moe, hop(give_moe, "expert", 1), slots)
    moe_result = return_plane(moe_partial)
    mixed_out = (resid_mid + join_halves(moe_result)).astype(brain_float_half)

    expert_pieces = scatter_line(expert_wgrad(*[list(part) for part in zip(*saved)]))

    grad_final = cotangent.astype(single_float)
    owner = (e_index ^ jnp.arange(expert_count))[:, None, None]
    grad_gates = jnp.sum(
        jnp.where(routes.T[None] == owner, gg_all[:, None, :], 0.0), axis=0
    ).T
    grad_picked = gates * (grad_gates - jnp.sum(gates * grad_gates, axis=-1, keepdims=True))
    grad_logits = jnp.sum(grad_picked[:, :, None] * chosen, axis=1).astype(brain_float_half)
    grad_router_w = lax.dot_general(
        grad_logits, normed_two, (((0,), (0,)), ((), ())), preferred_element_type=single_float
    )
    grad_normed_two = jnp.dot(grad_logits, router_w.T, preferred_element_type=single_float)
    grad_normed_two = grad_normed_two + join_halves(grad_result)
    scaled_two = grad_normed_two * gain_second
    grad_gain_two = jnp.sum(grad_normed_two * resid_mid * inverse_two, axis=0)
    grad_mid = (
        grad_final
        + inverse_two * scaled_two
        - resid_mid
        * inverse_two
        * inverse_two
        * inverse_two
        * jnp.mean(resid_mid * scaled_two, axis=-1, keepdims=True)
    )
    grad_mid_low = grad_mid.astype(brain_float_half)
    grad_out_w = jnp.dot(attn_rows.T, grad_mid_low, preferred_element_type=single_float)
    grad_attn = (
        lax.dot_general(
            grad_mid_low, out_w, (((1,), (1,)), ((), ())), preferred_element_type=single_float
        )
        .astype(brain_float_half)
        .reshape(count_of_rows, KEY_VALUE_HEADS, group_factor, HEAD_DIMENSION)
    )
    grad_out_part = reduce_weight(grad_out_w.astype(BF16))
    small_grads = reduce_small(jnp.concatenate([grad_gain_two[None], grad_router_w], axis=0))
    scores_again = masked_scores()
    probs_again = jnp.exp(scores_again - log_total)
    grad_probs = jnp.einsum(
        "qcgd,kcd->cgqk", grad_attn, value_row_block, preferred_element_type=single_float
    )
    delta_rows = jnp.sum(probs_again * grad_probs, axis=-1, keepdims=True)
    grad_scores = (probs_again * (grad_probs - delta_rows)).astype(brain_float_half)
    grad_query = (
        jnp.einsum(
            "cgqk,kcd->qcgd", grad_scores, key_row_block, preferred_element_type=single_float
        )
        * scale
    ).reshape(count_of_rows, QUERY_HEADS, HEAD_DIMENSION)
    key_matrix_gradient = (
        jnp.einsum(
            "cgqk,qcgd->kcd", grad_scores, query_vectors, preferred_element_type=single_float
        )
        * scale
    )
    value_matrix_gradient = jnp.einsum(
        "cgqk,qcgd->kcd",
        probs_again.astype(brain_float_half),
        grad_attn,
        preferred_element_type=single_float,
    )
    grad_query_pre = (
        reverse_rotary(grad_query, cosine_table, sine_table)
        .reshape(count_of_rows, QUERY_HEADS * HEAD_DIMENSION)
        .astype(brain_float_half)
    )
    key_before_gradient = (
        reverse_rotary(key_matrix_gradient, cosine_table, sine_table)
        .reshape(count_of_rows, KEY_VALUE_HEADS * HEAD_DIMENSION)
        .astype(brain_float_half)
    )
    value_before_gradient = value_matrix_gradient.reshape(
        count_of_rows, KEY_VALUE_HEADS * HEAD_DIMENSION
    ).astype(brain_float_half)
    grad_qkv = jnp.concatenate(
        [grad_query_pre, key_before_gradient, value_before_gradient], axis=1
    )
    grad_qkv_w = lax.dot_general(
        first_normalized, grad_qkv, (((0,), (0,)), ((), ())), preferred_element_type=single_float
    )
    qkv_part = reduce_weight(grad_qkv_w.astype(BF16))
    grad_normed_one = lax.dot_general(
        grad_qkv, qkv_w, (((1,), (1,)), ((), ())), preferred_element_type=single_float
    )
    scaled_one = grad_normed_one * gain_first
    grad_gain_one = jnp.sum(grad_normed_one * resid_in * inverse_one, axis=0)
    grad_input = (
        grad_mid
        + inverse_one * scaled_one
        - resid_in
        * inverse_one
        * inverse_one
        * inverse_one
        * jnp.mean(resid_in * scaled_one, axis=-1, keepdims=True)
    )
    gain_one_all = reduce_small(grad_gain_one[None])

    def own_part(values):
        return lax.dynamic_slice_in_dim(values, z_index * shard_rows, shard_rows, 1)

    small_part = own_part(small_grads)
    gate_rows = model_width // devices
    hidden = down_w.shape[0]
    return (
        mixed_out,
        grad_input.astype(brain_float_half),
        own_part(gain_one_all)[0],
        qkv_part[:, :query_width],
        qkv_part[:, query_width : query_width + key_width],
        qkv_part[:, query_width + key_width :],
        grad_out_part,
        small_part[0],
        small_part[1:].T,
        expert_pieces[None, :gate_rows, :hidden],
        expert_pieces[None, :gate_rows, hidden:],
        expert_pieces[None, gate_rows:, :],
    )


def solution(mesh):
    placed = (
        P(("dp", "expert"), None),
        P(("dp", "expert"), None),
        P(("dp", "expert"), None),
        P(("dp", "expert"), None),
        P("dp"),
        P("dp", None),
        P("dp", None),
        P("dp", None),
        P("dp", None),
        P("dp"),
        P("dp", None),
        P("expert", None, None),
        P("expert", None, None),
        P("expert", None, None),
    )
    return jax.shard_map(
        local,
        mesh=mesh,
        in_specs=placed,
        out_specs=(
            P(("dp", "expert"), None),
            P(("dp", "expert"), None),
            P("dp"),
            P("dp", None),
            P("dp", None),
            P("dp", None),
            P("dp", None),
            P("dp"),
            P("dp", None),
            P("expert", "dp", None),
            P("expert", "dp", None),
            P("expert", "dp", None),
        ),
        check_vma=False,
    )
```

time: 759 us -> 716 us (0.943)
  Pallas kernels: 0 us -> 270 us
  blocking collectives: 161 us -> 0 us
  waiting for transfers between devices: 289 us -> 152 us
  starting transfers between devices: 10.3 us -> 121 us
  matrix products: 136 us -> 63.7 us
  local copies, waits for them, and re-layouts: 71.9 us -> 35.9 us
  between operations: 16 us -> 3.05 us
  other arithmetic: 70.7 us -> 62.2 us
    pallas_call x0 -> x15, Pallas kernels: none -> 270 us  [the longest x2 194 us: gather_weight(): pl.pallas_call(lambda *refs: place_kernel(devices, count, rows, *refs), o...]
    ppermute x0 -> x137, waiting for transfers between devices: none -> 152 us  [the longest x131 150 us: hop(): return lax.ppermute(values, axis, [(i, i ^ mask) for i in range(count)])]
    ppermute x0 -> x137, starting transfers between devices: none -> 121 us  [the longest x131 107 us: hop(): return lax.ppermute(values, axis, [(i, i ^ mask) for i in range(count)])]
    all_to_all x2 -> x0, blocking collectives: 105 us -> none  [the longest x1 52.8 us: local(): lax.all_to_all(outgoing, 'expert', split_axis=0, concat_axis=0, tiled=True)]
    reduce_scatter x8 -> x0, waiting for transfers between devices: 102 us -> none  [the longest x1 45.5 us: local(): lax.psum_scatter(grad_query_w.astype(jnp.bfloat16), 'dp', scatter_dimensi...]
    all_gather x4 -> x0, waiting for transfers between devices: 84 us -> none  [the longest x1 44.2 us: local(): lax.all_gather(w_query, 'dp', axis=0, tiled=True)]
    dot_general x24 -> x7, matrix products: 83.5 us -> 11.9 us  [the longest x1 4.6 us: local(): qkv = jnp.dot(first_normalized, qkv_w, preferred_element_type=single_float)]
    all_to_all x2 -> x0, waiting for transfers between devices: 56.8 us -> none  [the longest x1 32.9 us: local(): lax.all_to_all(grad_send, 'expert', split_axis=0, concat_axis=0, tiled=True)]
  transfers between devices with their start and end apart: 15 -> 137, of which waited for: 10 -> 46; matrix products, arithmetic and copies ran while one was open for 25% -> 21% of each run, Pallas kernels for 0% -> 20%
where the time goes in v1:
time: 716 us; the launch traced here: 708 us
  Pallas kernels  270 us (38%)
  waiting for transfers between devices  152 us (21%)
  starting transfers between devices  121 us (17%)
  matrix products  63.7 us (9%)
  other arithmetic  62.2 us (9%)
  local copies, waits for them, and re-layouts  35.9 us (5%)
    pallas_call x2, Pallas kernels, gather_weight(): pl.pallas_call(lambda *refs: place_kernel(devices, count, rows, *refs), o...  194 us
    ppermute x131, waiting for transfers between devices, hop(): return lax.ppermute(values, axis, [(i, i ^ mask) for i in range(count)])  150 us
    ppermute x131, starting transfers between devices, hop(): return lax.ppermute(values, axis, [(i, i ^ mask) for i in range(count)])  107 us
    pallas_call x4, Pallas kernels, expert_group(): pl.pallas_call(lambda *refs: expert_kernel(capacity, *refs), out_shape=(l...  41.3 us
    pallas_call x8, Pallas kernels, combine(): pl.pallas_call(lambda *refs: combine_kernel(capacity, *refs), out_shape=(...  22.1 us
  transfers between devices with their start and end apart: 137, of which 46 were waited for; matrix products, arithmetic and copies ran while one was open for 21% of the time, Pallas kernels for 20%

profile of v1, /device:TPU:0, one launch (start us, length us, event | category | flops | bytes accessed | tf_op | source)
XLA Modules:
  0.0 707.6 jit_solution(1438420081428501575)
XLA Ops:
  2.8 3.1 collective-permute-start
  9.9 3.8 collective-permute-start.22
  25.4 3.8 collective-permute-start.5
  68.2 2.8 collective-permute-done.11.refs_6_
  71.7 65.1 %place_weight.3 = bf16[1024,1024]{1,0:T(8,128)(2,1)} custom-call(bf16[96,512]{1,0:T(8,128)(2,1)} %copy-done.39, bf16[96,512]{1,0:T(8,128)(2,1)} %copy-done.63, bf16[96,512]{1,0:T(8,128)(2,1)} %copy-done.62, bf16[96,512]{1,0:T(8,128)(2,1)} %copy-done.67, bf16[96,512]{1,0:T(8,128)(2,1)} %copy-done.61, bf16[96,512]{1,0:T(8,128)(2,1)} %collective-permute-done.27.refs_5_, ...), custom_call_target="tpu_custom_call" | custom-call | tf_op jit(solution)/shard_map/place_weight/pallas_call | solution.py:149
  137.0 128.6 %place_weight.2 = bf16[1024,2048]{1,0:T(8,128)(2,1)} custom-call(bf16[96,1024]{1,0:T(8,128)(2,1)} %copy-done.28, bf16[96,1024]{1,0:T(8,128)(2,1)} %copy-done.48, bf16[96,1024]{1,0:T(8,128)(2,1)} %copy-done.47, bf16[96,1024]{1,0:T(8,128)(2,1)} %collective-permute-done.8.refs_3_, bf16[96,1024]{1,0:T(8,128)(2,1)} %copy-done.46, ...), custom_call_target="tpu_custom_call" | custom-call | tf_op jit(solution)/shard_map/place_weight/pallas_call | solution.py:149
  269.8 4.6 fusion.40
  284.1 7.2 %fusion.109 = (f32[8,2,512]{2,1,0:T(2,128)S(1)}, f32[8,2,512,512]{2,3,1,0:T(8,128)}) fusion(bf16[512,8,2,32]{0,3,2,1:T(8,128)(2,1)S(1)} %bitcast.204, bf16[512,8,2,32]{0,3,2,1:T(8,128)(2,1)S(1)} %bitcast.202, bf16[512,8,32]{0,2,1:T(8,128)(2,1)S(1)} %get-tuple-element.151, bf16[512,8,32]{0,2,1:T(8,128)(2,1)S(1)} %get-tuple-element.150, ...), kind=kOutput, calls=%fused_computation.271 | convolution fusion | flops 552591360 | bytes 18644992 | tf_op jit(solution)/shard_map/qcgd,kcd->cgqk/dot_general | solution.py:569
  291.4 8.3 %fusion.3 = f32[8,2,512]{2,1,0:T(2,128)S(1)} fusion(f32[8,2,512,512]{2,3,1,0:T(8,128)} %get-tuple-element.201, f32[8,2,512]{2,1,0:T(2,128)S(1)} %get-tuple-element.200), kind=kLoop, calls=%fused_computation.10 | loop fusion | flops 8380416 | bytes 16842752 | tf_op jit(solution)/shard_map/reduce_sum | solution.py:579
  299.8 8.1 %fusion.24 = bf16[8,64,2,512]{3,1,2,0:T(8,128)(2,1)S(1)} fusion(bf16[512,8,64,1]{0,2,3,1:T(8,128)(2,1)S(1)} %bitcast.200, f32[8,2,512,512]{2,3,1,0:T(8,128)} %get-tuple-element.201, f32[8,2,512]{2,1,0:T(2,128)S(1)} %fusion.3, f32[8,2,512]{2,1,0:T(2,128)S(1)} %get-tuple-element.200), kind=kOutput, calls=%fused_computation.54 | convolution fusion | flops 549978112 | bytes 18415616 | tf_op jit(solution)/shard_map/cgqk,kcd->qcgd/dot_general | solution.py:582
  315.9 8.9 %collective-permute-done.66.refs_1_ = bf16[256,1024]{1,0:T(8,128)(2,1)} collective-permute-done((bf16[256,1024]{1,0:T(8,128)(2,1)S(1)}, bf16[256,1024]{1,0:T(8,128)(2,1)}, u32[]{:S(2)}, u32[]{:S(2)}) %collective-permute-start.66) | collective-permute-done | bytes 524320 | tf_op jit(solution)/shard_map/ppermute | solution.py:66
  329.1 6.4 collective-permute-done.53.refs_0_
  339.1 9.0 %collective-permute-done.59.refs_4_ = bf16[256,1024]{1,0:T(8,128)(2,1)} collective-permute-done((bf16[256,1024]{1,0:T(8,128)(2,1)}, bf16[256,1024]{1,0:T(8,128)(2,1)}, u32[]{:S(2)}, u32[]{:S(2)}) %collective-permute-start.59) | collective-permute-done | bytes 524320 | tf_op jit(solution)/shard_map/ppermute | solution.py:66
  351.7 10.3 %expert_group.4 = (bf16[256,1024]{1,0:T(8,128)(2,1)}, bf16[256,1024]{1,0:T(8,128)(2,1)}, bf16[256,1024]{1,0:T(8,128)(2,1)}, bf16[256,1024]{1,0:T(8,128)(2,1)}, b...) custom-call(bf16[256,1024]{1,0:T(8,128)(2,1)} %copy-done.37, ...), custom_call_target="tpu_custom_call" | custom-call | flops 4294967296 | bytes 16777216 | tf_op jit(solution)/shard_map/expert_group/pallas_call | solution.py:331
  366.3 10.4 %expert_group.7 = (bf16[256,1024]{1,0:T(8,128)(2,1)}, bf16[256,1024]{1,0:T(8,128)(2,1)}, bf16[256,1024]{1,0:T(8,128)(2,1)}, bf16[256,1024]{1,0:T(8,128)(2,1)}, b...) custom-call(bf16[256,1024]{1,0:T(8,128)(2,1)} %copy-done.102, ...), custom_call_target="tpu_custom_call" | custom-call | flops 4294967296 | bytes 16777216 | tf_op jit(solution)/shard_map/expert_group/pallas_call | solution.py:331
  377.9 10.2 %expert_group.5 = (bf16[256,1024]{1,0:T(8,128)(2,1)}, bf16[256,1024]{1,0:T(8,128)(2,1)}, bf16[256,1024]{1,0:T(8,128)(2,1)}, bf16[256,1024]{1,0:T(8,128)(2,1)}, b...) custom-call(bf16[256,1024]{1,0:T(8,128)(2,1)} %copy-done.99, ...), custom_call_target="tpu_custom_call" | custom-call | flops 4294967296 | bytes 16777216 | tf_op jit(solution)/shard_map/expert_group/pallas_call | solution.py:331
  388.4 2.7 combine_rows.15
  393.8 10.4 %expert_group.6 = (bf16[256,1024]{1,0:T(8,128)(2,1)}, bf16[256,1024]{1,0:T(8,128)(2,1)}, bf16[256,1024]{1,0:T(8,128)(2,1)}, bf16[256,1024]{1,0:T(8,128)(2,1)}, b...) custom-call(bf16[256,1024]{1,0:T(8,128)(2,1)} %copy-done.105, ...), custom_call_target="tpu_custom_call" | custom-call | flops 4294967296 | bytes 16777216 | tf_op jit(solution)/shard_map/expert_group/pallas_call | solution.py:331
  404.6 12.5 %expert_wgrad.1 = bf16[4,384,1024]{2,1,0:T(8,128)(2,1)} custom-call(bf16[512,1024]{1,0:T(8,128)(2,1)} %get-tuple-element.112.refs_0_, bf16[512,1024]{1,0:T(8,128)(2,1)} %get-tuple-element.113.refs_1_, bf16[512,1024]{1,0:T(8,128)(2,1)} %get-tuple-element.114.refs_2_, bf16[512,1024]{1,0:T(8,128)(2,1)} %get-tuple-element.115.refs_3_, ...), custom_call_target="tpu_custom_call" | custom-call | flops 6442450944 | bytes 16777216 | tf_op jit(solution)/shard_map/expert_wgrad/pallas_call | solution.py:428
  420.3 2.7 combine_rows.8
  427.4 2.7 combine_rows.10
  436.7 2.8 combine_rows.9
  442.9 13.0 %collective-permute-done.73 = bf16[256,1024]{1,0:T(8,128)(2,1)S(1)} collective-permute-done((bf16[256,1024]{1,0:T(8,128)(2,1)}, bf16[256,1024]{1,0:T(8,128)(2,1)S(1)}, u32[]{:S(2)}, u32[]{:S(2)}) %collective-permute-start.73) | collective-permute-done | bytes 524320 | tf_op jit(solution)/shard_map/ppermute | solution.py:66
  459.1 10.6 %collective-permute-done.74 = bf16[256,1024]{1,0:T(8,128)(2,1)S(1)} collective-permute-done((bf16[256,1024]{1,0:T(8,128)(2,1)S(1)}, bf16[256,1024]{1,0:T(8,128)(2,1)S(1)}, u32[]{:S(2)}, u32[]{:S(2)}) %collective-permute-start.74) | collective-permute-done | bytes 524320 | tf_op jit(solution)/shard_map/ppermute | solution.py:66
  472.5 2.7 multiply_reduce_fusion
  481.1 3.1 collective-permute-done.127
  490.0 7.4 %collective-permute-done.129 = f32[9,1024]{1,0:T(8,128)S(1)} collective-permute-done((f32[9,1024]{1,0:T(8,128)S(1)}, f32[9,1024]{1,0:T(8,128)S(1)}, u32[]{:S(2)}, u32[]{:S(2)}) %collective-permute-start.129) | collective-permute-done | bytes 36896 | tf_op jit(solution)/shard_map/ppermute | solution.py:66
  497.6 2.7 combine_rows.14
  501.6 2.7 add_convert_fusion.3
  506.8 2.8 combine_rows.11
  509.6 5.7 collective-permute-start.133
  515.3 2.7 combine_rows.12
  519.3 2.7 combine_rows.13
  528.9 4.3 collective-permute-done.77
  534.7 12.0 %collective-permute-done.81 = bf16[256,1024]{1,0:T(8,128)(2,1)S(1)} collective-permute-done((bf16[256,1024]{1,0:T(8,128)(2,1)S(1)}, bf16[256,1024]{1,0:T(8,128)(2,1)S(1)}, u32[]{:S(2)}, u32[]{:S(2)}) %collective-permute-start.81) | collective-permute-done | bytes 524320 | tf_op jit(solution)/shard_map/ppermute | solution.py:66
  555.6 8.6 %fusion.30 = bf16[8,64,512]{2,1,0:T(8,128)(2,1)S(1)} fusion(bf16[512,8,2,64]{0,3,2,1:T(8,128)(2,1)S(1)} %bitcast.189, f32[8,2,512,512]{2,3,1,0:T(8,128)} %get-tuple-element.201, f32[8,2,512]{2,1,0:T(2,128)S(1)} %bitcast.221), kind=kOutput, calls=%fused_computation.60 | convolution fusion | flops 545521664 | bytes 18382848 | tf_op jit(solution)/shard_map/cgqk,qcgd->kcd/dot_general | solution.py:689
  564.2 13.2 %fusion = (f32[8,2,512]{2,1,0:T(2,128)S(1)}, f32[8,512,512,2]{2,1,3,0:T(8,128)}) fusion(f32[8,2,512,512]{2,3,1,0:T(8,128)} %get-tuple-element.201, f32[8,2,512]{2,1,0:T(2,128)S(1)} %bitcast.222, bf16[512,8,64,1]{0,2,3,1:T(8,128)(2,1)S(1)} %bitcast.201, bf16[512,8,2,64]{0,3,2,1:T(8,128)(2,1)S(1)} %bitcast.190), kind=kOutput, calls=%fused_computation.3 | convolution fusion | flops 549445632 | bytes 35192832 | tf_op jit(solution)/shard_map/qcgd,kcd->cgqk/dot_general | solution.py:672
  577.5 11.0 %fusion.2 = bf16[8,2,512,512]{2,3,1,0:T(8,128)(2,1)} fusion(f32[8,512,512,2]{2,1,3,0:T(8,128)} %get-tuple-element.206, f32[8,2,512,512]{2,3,1,0:T(8,128)S(1)} %bitcast.188, f32[8,2,512]{2,1,0:T(2,128)S(1)} %get-tuple-element.205, f32[8,2,512]{2,1,0:T(2,128)S(1)} %bitcast.223), kind=kLoop, calls=%fused_computation.5 | loop fusion | flops 16777216 | bytes 42008576 | tf_op jit(solution)/shard_map/convert_element_type | solution.py:676
  588.5 6.2 fusion.29
  599.2 2.7 fusion.19
  602.5 2.6 convolution_convert_fusion
  626.9 3.5 collective-permute-done.116
  631.8 3.7 collective-permute-done.117
  635.7 2.7 collective-permute-start.118
  649.8 11.1 %collective-permute-done.101 = bf16[2,2,1,1,32,2048]{5,4,3,2,1,0:T(8,128)(2,1)S(1)} collective-permute-done((bf16[2,2,1,1,32,2048]{5,4,3,2,1,0:T(8,128)(2,1)S(1)}, bf16[2,2,1,1,32,2048]{5,4,3,2,1,0:T(8,128)(2,1)S(1)}, u32[]{:S(2)}, u32[]{:S(2)}) %collective-permute-start.101) | collective-permute-done | bytes 524320 | tf_op jit(solution)/shard_map/ppermute | solution.py:66
  664.1 5.0 collective-permute-done.102
  678.2 5.3 collective-permute-done.106
  695.0 3.4 collective-permute-done.109
  (662 shorter events, 228.4 us)
Async XLA Ops:
  2.8 22.0 %collective-permute-start = (bf16[16,256]{1,0:T(8,128)(2,1)S(1)}, bf16[16,256]{1,0:T(8,128)(2,1)S(1)}, u32[]{:S(2)}, u32[]{:S(2)}) collective-permute-start(bf16[16,256]{1,0:T(8,128)(2,1)S(1)} %fusion.70), channel_id=1, source_target_pairs={{0,8},{8,0},{16,24},{24,16},{1,9},{9,1},{17,25},{25,17},{2,10},{10... | collective-permute-start | bytes 24584 | tf_op jit(solution)/shard_map/ppermute | solution.py:66
  5.9 19.5 %collective-permute-start.1 = (bf16[16,256]{1,0:T(8,128)(2,1)S(1)}, bf16[16,256]{1,0:T(8,128)(2,1)S(1)}, u32[]{:S(2)}, u32[]{:S(2)}) collective-permute-start(bf16[16,256]{1,0:T(8,128)(2,1)S(1)} %fusion.70), channel_id=1, source_target_pairs={{0,16},{8,24},{16,0},{24,8},{1,17},{9,25},{17,1},{25,9},{2,18},{10... | collective-permute-start | bytes 24584 | tf_op jit(solution)/shard_map/ppermute | solution.py:66
  8.5 20.7 %collective-permute-start.2 = (bf16[16,256]{1,0:T(8,128)(2,1)S(1)}, bf16[16,256]{1,0:T(8,128)(2,1)S(1)}, u32[]{:S(2)}, u32[]{:S(2)}) collective-permute-start(bf16[16,256]{1,0:T(8,128)(2,1)S(1)} %fusion.70), channel_id=1, source_target_pairs={{0,24},{8,16},{16,8},{24,0},{1,25},{9,17},{17,9},{25,1},{2,26},{10... | collective-permute-start | bytes 24584 | tf_op jit(solution)/shard_map/ppermute | solution.py:66
  8.5 16.3 %collective-permute-start.41 = (s32[1,2,512]{2,1,0:T(2,128)}, s32[1,2,512]{2,1,0:T(2,128)S(1)}, u32[]{:S(2)}, u32[]{:S(2)}) collective-permute-start(s32[1,2,512]{2,1,0:T(2,128)} %bitcast.226), channel_id=1, source_target_pairs={{0,1},{1,0},{2,3},{3,2},{4,5},{5,4},{6,7},{7,6},{8,9},{9,8},{10,11... | collective-permute-start | bytes 12296 | tf_op jit(solution)/shard_map/ppermute | solution.py:66
  9.9 25.3 %collective-permute-start.22 = (bf16[32,1024]{1,0:T(8,128)(2,1)}, bf16[32,1024]{1,0:T(8,128)(2,1)}, u32[]{:S(2)}, u32[]{:S(2)}) collective-permute-start(bf16[32,1024]{1,0:T(8,128)(2,1)} %constant_dynamic-slice_fusion.12), channel_id=1, source_target_pairs={{0,24},{8,16},{16,8},{24,0},{1,25},{9,17},{17,9},{25,1},{2,26},{10... | collective-permute-start | bytes 196616 | tf_op jit(solution)/shard_map/ppermute | solution.py:66
  25.4 15.9 %collective-permute-start.5 = (bf16[32,2048]{1,0:T(8,128)(2,1)S(1)}, bf16[32,2048]{1,0:T(8,128)(2,1)S(1)}, u32[]{:S(2)}, u32[]{:S(2)}) collective-permute-start(bf16[32,2048]{1,0:T(8,128)(2,1)S(1)} %constant_dynamic-slice_fusion.13), channel_id=1, source_target_pairs={{0,24},{8,16},{16,8},{24,0},{1,25},{9,17},{17,9},{25,1},{2,26},{10... | collective-permute-start | bytes 393224 | tf_op jit(solution)/shard_map/ppermute | solution.py:66
  65.0 72.0 %collective-permute-start.8 = (bf16[96,1024]{1,0:T(8,128)(2,1)S(1)}, bf16[96,1024]{1,0:T(8,128)(2,1)}, u32[]{:S(2)}, u32[]{:S(2)}) collective-permute-start(bf16[96,1024]{1,0:T(8,128)(2,1)S(1)} %collective-permute-done.7.refs_2_), channel_id=1, source_target_pairs={{0,1},{1,0},{2,3},{3,2},{4,5},{5,4},{6,7},{7,6},{8,9},{9,8},{10,11... | collective-permute-start | bytes 589832 | tf_op jit(solution)/shard_map/ppermute | solution.py:66
  65.2 71.8 %collective-permute-start.15 = (bf16[96,1024]{1,0:T(8,128)(2,1)S(1)}, bf16[96,1024]{1,0:T(8,128)(2,1)}, u32[]{:S(2)}, u32[]{:S(2)}) collective-permute-start(bf16[96,1024]{1,0:T(8,128)(2,1)S(1)} %collective-permute-done.14.refs_10_), channel_id=1, source_target_pairs={{0,1},{1,0},{2,3},{3,2},{4,5},{5,4},{6,7},{7,6},{8,9},{9,8},{10,11... | collective-permute-start | bytes 589832 | tf_op jit(solution)/shard_map/ppermute | solution.py:66
  67.7 69.3 %collective-permute-start.10 = (bf16[96,1024]{1,0:T(8,128)(2,1)S(1)}, bf16[96,1024]{1,0:T(8,128)(2,1)}, u32[]{:S(2)}, u32[]{:S(2)}) collective-permute-start(bf16[96,1024]{1,0:T(8,128)(2,1)S(1)} %collective-permute-done.9.refs_4_), channel_id=1, source_target_pairs={{0,1},{1,0},{2,3},{3,2},{4,5},{5,4},{6,7},{7,6},{8,9},{9,8},{10,11... | collective-permute-start | bytes 589832 | tf_op jit(solution)/shard_map/ppermute | solution.py:66
  67.7 69.3 %collective-permute-start.19 = (bf16[96,1024]{1,0:T(8,128)(2,1)S(1)}, bf16[96,1024]{1,0:T(8,128)(2,1)}, u32[]{:S(2)}, u32[]{:S(2)}) collective-permute-start(bf16[96,1024]{1,0:T(8,128)(2,1)S(1)} %collective-permute-done.18.refs_14_), channel_id=1, source_target_pairs={{0,1},{1,0},{2,3},{3,2},{4,5},{5,4},{6,7},{7,6},{8,9},{9,8},{10,11... | collective-permute-start | bytes 589832 | tf_op jit(solution)/shard_map/ppermute | solution.py:66
  71.0 66.1 %collective-permute-start.12 = (bf16[96,1024]{1,0:T(8,128)(2,1)}, bf16[96,1024]{1,0:T(8,128)(2,1)}, u32[]{:S(2)}, u32[]{:S(2)}) collective-permute-start(bf16[96,1024]{1,0:T(8,128)(2,1)} %collective-permute-done.11.refs_6_), channel_id=1, source_target_pairs={{0,1},{1,0},{2,3},{3,2},{4,5},{5,4},{6,7},{7,6},{8,9},{9,8},{10,11... | collective-permute-start | bytes 589832 | tf_op jit(solution)/shard_map/ppermute | solution.py:66
  265.7 44.2 %collective-permute-start.58 = (bf16[256,1024]{1,0:T(8,128)(2,1)}, bf16[256,1024]{1,0:T(8,128)(2,1)}, u32[]{:S(2)}, u32[]{:S(2)}) collective-permute-start(bf16[256,1024]{1,0:T(8,128)(2,1)} %get-tuple-element.70.refs_4_), channel_id=1, source_target_pairs={{0,2},{1,3},{2,0},{3,1},{4,6},{5,7},{6,4},{7,5},{8,10},{9,11},{10,... | collective-permute-start | bytes 1572872 | tf_op jit(solution)/shard_map/ppermute | solution.py:66
  267.2 42.7 %collective-permute-start.48 = (bf16[256,1024]{1,0:T(8,128)(2,1)}, bf16[256,1024]{1,0:T(8,128)(2,1)}, u32[]{:S(2)}, u32[]{:S(2)}) collective-permute-start(bf16[256,1024]{1,0:T(8,128)(2,1)} %get-tuple-element.70.refs_4_), channel_id=1, source_target_pairs={{0,4},{1,5},{2,6},{3,7},{4,0},{5,1},{6,2},{7,3},{8,12},{9,13},{10,... | collective-permute-start | bytes 1572872 | tf_op jit(solution)/shard_map/ppermute | solution.py:66
  268.7 42.8 %collective-permute-start.39 = (bf16[256,1024]{1,0:T(8,128)(2,1)}, bf16[256,1024]{1,0:T(8,128)(2,1)}, u32[]{:S(2)}, u32[]{:S(2)}) collective-permute-start(bf16[256,1024]{1,0:T(8,128)(2,1)} %get-tuple-element.70.refs_4_), channel_id=1, source_target_pairs={{0,1},{1,0},{2,3},{3,2},{4,5},{5,4},{6,7},{7,6},{8,9},{9,8},{10,11... | collective-permute-start | bytes 1572872 | tf_op jit(solution)/shard_map/ppermute | solution.py:66
  268.7 44.3 %collective-permute-start.69 = (bf16[256,1024]{1,0:T(8,128)(2,1)}, bf16[256,1024]{1,0:T(8,128)(2,1)}, u32[]{:S(2)}, u32[]{:S(2)}) collective-permute-start(bf16[256,1024]{1,0:T(8,128)(2,1)} %get-tuple-element.71.refs_5_), channel_id=1, source_target_pairs={{0,2},{1,3},{2,0},{3,1},{4,6},{5,7},{6,4},{7,5},{8,10},{9,11},{10,... | collective-permute-start | bytes 1572872 | tf_op jit(solution)/shard_map/ppermute | solution.py:66
  269.0 44.6 %collective-permute-start.49 = (bf16[256,1024]{1,0:T(8,128)(2,1)}, bf16[256,1024]{1,0:T(8,128)(2,1)}, u32[]{:S(2)}, u32[]{:S(2)}) collective-permute-start(bf16[256,1024]{1,0:T(8,128)(2,1)} %get-tuple-element.71.refs_5_), channel_id=1, source_target_pairs={{0,4},{1,5},{2,6},{3,7},{4,0},{5,1},{6,2},{7,3},{8,12},{9,13},{10,... | collective-permute-start | bytes 1572872 | tf_op jit(solution)/shard_map/ppermute | solution.py:66
  313.6 21.9 %collective-permute-start.53 = (bf16[256,1024]{1,0:T(8,128)(2,1)S(1)}, bf16[256,1024]{1,0:T(8,128)(2,1)S(1)}, u32[]{:S(2)}, u32[]{:S(2)}) collective-permute-start(bf16[256,1024]{1,0:T(8,128)(2,1)S(1)} %get-tuple-element.159.refs_0_), channel_id=1, source_target_pairs={{0,2},{1,3},{2,0},{3,1},{4,6},{5,7},{6,4},{7,5},{8,10},{9,11},{10,... | collective-permute-start | bytes 1572872 | tf_op jit(solution)/shard_map/ppermute | solution.py:66
  315.1 22.4 %collective-permute-start.44 = (bf16[256,1024]{1,0:T(8,128)(2,1)S(1)}, bf16[256,1024]{1,0:T(8,128)(2,1)S(1)}, u32[]{:S(2)}, u32[]{:S(2)}) collective-permute-start(bf16[256,1024]{1,0:T(8,128)(2,1)S(1)} %get-tuple-element.159.refs_0_), channel_id=1, source_target_pairs={{0,4},{1,5},{2,6},{3,7},{4,0},{5,1},{6,2},{7,3},{8,12},{9,13},{10,... | collective-permute-start | bytes 1572872 | tf_op jit(solution)/shard_map/ppermute | solution.py:66
  326.3 21.8 %collective-permute-start.59 = (bf16[256,1024]{1,0:T(8,128)(2,1)}, bf16[256,1024]{1,0:T(8,128)(2,1)}, u32[]{:S(2)}, u32[]{:S(2)}) collective-permute-start(bf16[256,1024]{1,0:T(8,128)(2,1)} %collective-permute-done.58.refs_4_), channel_id=1, source_target_pairs={{0,4},{1,5},{2,6},{3,7},{4,0},{5,1},{6,2},{7,3},{8,12},{9,13},{10,... | collective-permute-start | bytes 1572872 | tf_op jit(solution)/shard_map/ppermute | solution.py:66
  337.5 25.1 %collective-permute-start.60 = (bf16[256,1024]{1,0:T(8,128)(2,1)}, bf16[256,1024]{1,0:T(8,128)(2,1)}, u32[]{:S(2)}, u32[]{:S(2)}) collective-permute-start(bf16[256,1024]{1,0:T(8,128)(2,1)} %collective-permute-done.49.refs_5_), channel_id=1, source_target_pairs={{0,2},{1,3},{2,0},{3,1},{4,6},{5,7},{6,4},{7,5},{8,10},{9,11},{10,... | collective-permute-start | bytes 1572872 | tf_op jit(solution)/shard_map/ppermute | solution.py:66
  338.1 24.6 %collective-permute-start.51 = (bf16[256,1024]{1,0:T(8,128)(2,1)}, bf16[256,1024]{1,0:T(8,128)(2,1)}, u32[]{:S(2)}, u32[]{:S(2)}) collective-permute-start(bf16[256,1024]{1,0:T(8,128)(2,1)} %collective-permute-done.49.refs_5_), channel_id=1, source_target_pairs={{0,1},{1,0},{2,3},{3,2},{4,5},{5,4},{6,7},{7,6},{8,9},{9,8},{10,11... | collective-permute-start | bytes 1572872 | tf_op jit(solution)/shard_map/ppermute | solution.py:66
  338.3 23.7 %collective-permute-start.71 = (bf16[256,1024]{1,0:T(8,128)(2,1)}, bf16[256,1024]{1,0:T(8,128)(2,1)}, u32[]{:S(2)}, u32[]{:S(2)}) collective-permute-start(bf16[256,1024]{1,0:T(8,128)(2,1)} %collective-permute-done.69.refs_5_), channel_id=1, source_target_pairs={{0,1},{1,0},{2,3},{3,2},{4,5},{5,4},{6,7},{7,6},{8,9},{9,8},{10,11... | collective-permute-start | bytes 1572872 | tf_op jit(solution)/shard_map/ppermute | solution.py:66
  365.5 22.6 %collective-permute-start.92 = (bf16[256,1024]{1,0:T(8,128)(2,1)}, bf16[256,1024]{1,0:T(8,128)(2,1)}, u32[]{:S(2)}, u32[]{:S(2)}) collective-permute-start(bf16[256,1024]{1,0:T(8,128)(2,1)} %get-tuple-element.107), channel_id=1, source_target_pairs={{0,1},{1,0},{2,3},{3,2},{4,5},{5,4},{6,7},{7,6},{8,9},{9,8},{10,11... | collective-permute-start | bytes 1572872 | tf_op jit(solution)/shard_map/ppermute | solution.py:66
  388.1 34.9 %collective-permute-start.85 = (f32[512]{0:T(512)S(1)}, f32[512]{0:T(512)}, u32[]{:S(2)}, u32[]{:S(2)}) collective-permute-start(f32[512]{0:T(512)S(1)} %bitcast.249), channel_id=1, source_target_pairs={{0,1},{1,0},{2,3},{3,2},{4,5},{5,4},{6,7},{7,6},{8,9},{9,8},{10,11... | collective-permute-start | bytes 6152 | tf_op jit(solution)/shard_map/ppermute | solution.py:66
  392.0 32.8 %collective-permute-start.88 = (f32[512]{0:T(512)S(1)}, f32[512]{0:T(512)}, u32[]{:S(2)}, u32[]{:S(2)}) collective-permute-start(f32[512]{0:T(512)S(1)} %bitcast.253), channel_id=1, source_target_pairs={{0,4},{1,5},{2,6},{3,7},{4,0},{5,1},{6,2},{7,3},{8,12},{9,13},{10,... | collective-permute-start | bytes 6152 | tf_op jit(solution)/shard_map/ppermute | solution.py:66
  392.8 26.3 %collective-permute-start.52 = (bf16[256,1024]{1,0:T(8,128)(2,1)}, bf16[256,1024]{1,0:T(8,128)(2,1)S(1)}, u32[]{:S(2)}, u32[]{:S(2)}) collective-permute-start(bf16[256,1024]{1,0:T(8,128)(2,1)} %get-tuple-element.75), channel_id=1, source_target_pairs={{0,1},{1,0},{2,3},{3,2},{4,5},{5,4},{6,7},{7,6},{8,9},{9,8},{10,11... | collective-permute-start | bytes 1572872 | tf_op jit(solution)/shard_map/ppermute | solution.py:66
  393.0 33.7 %collective-permute-start.72 = (bf16[256,1024]{1,0:T(8,128)(2,1)S(1)}, bf16[256,1024]{1,0:T(8,128)(2,1)S(1)}, u32[]{:S(2)}, u32[]{:S(2)}) collective-permute-start(bf16[256,1024]{1,0:T(8,128)(2,1)S(1)} %copy-done.101), channel_id=1, source_target_pairs={{0,1},{1,0},{2,3},{3,2},{4,5},{5,4},{6,7},{7,6},{8,9},{9,8},{10,11... | collective-permute-start | bytes 1572872 | tf_op jit(solution)/shard_map/ppermute | solution.py:66
  404.2 32.5 %collective-permute-start.63 = (bf16[256,1024]{1,0:T(8,128)(2,1)}, bf16[256,1024]{1,0:T(8,128)(2,1)}, u32[]{:S(2)}, u32[]{:S(2)}) collective-permute-start(bf16[256,1024]{1,0:T(8,128)(2,1)} %get-tuple-element.78), channel_id=1, source_target_pairs={{0,1},{1,0},{2,3},{3,2},{4,5},{5,4},{6,7},{7,6},{8,9},{9,8},{10,11... | collective-permute-start | bytes 1572872 | tf_op jit(solution)/shard_map/ppermute | solution.py:66
  430.2 28.9 %collective-permute-start.94 = (bf16[256,1024]{1,0:T(8,128)(2,1)}, bf16[256,1024]{1,0:T(8,128)(2,1)}, u32[]{:S(2)}, u32[]{:S(2)}) collective-permute-start(bf16[256,1024]{1,0:T(8,128)(2,1)} %get-tuple-element.111), channel_id=1, source_target_pairs={{0,4},{1,5},{2,6},{3,7},{4,0},{5,1},{6,2},{7,3},{8,12},{9,13},{10,... | collective-permute-start | bytes 1572872 | tf_op jit(solution)/shard_map/ppermute | solution.py:66
  431.5 39.5 %collective-permute-start.93 = (bf16[256,1024]{1,0:T(8,128)(2,1)}, bf16[256,1024]{1,0:T(8,128)(2,1)}, u32[]{:S(2)}, u32[]{:S(2)}) collective-permute-start(bf16[256,1024]{1,0:T(8,128)(2,1)} %get-tuple-element.109), channel_id=1, source_target_pairs={{0,2},{1,3},{2,0},{3,1},{4,6},{5,7},{6,4},{7,5},{8,10},{9,11},{10,... | collective-permute-start | bytes 1572872 | tf_op jit(solution)/shard_map/ppermute | solution.py:66
  432.8 42.5 %collective-permute-start.131 = (bf16[384,1024]{1,0:T(8,128)(2,1)}, bf16[384,1024]{1,0:T(8,128)(2,1)}, u32[]{:S(2)}, u32[]{:S(2)}) collective-permute-start(bf16[384,1024]{1,0:T(8,128)(2,1)} %dynamic-slice_bitcast_fusion), channel_id=1, source_target_pairs={{0,8},{1,9},{2,10},{3,11},{4,12},{5,13},{6,14},{7,15}} | collective-permute-start | bytes 2359304 | tf_op jit(solution)/shard_map/ppermute | solution.py:239
  439.5 16.4 %collective-permute-start.73 = (bf16[256,1024]{1,0:T(8,128)(2,1)}, bf16[256,1024]{1,0:T(8,128)(2,1)S(1)}, u32[]{:S(2)}, u32[]{:S(2)}) collective-permute-start(bf16[256,1024]{1,0:T(8,128)(2,1)} %get-tuple-element.83), channel_id=1, source_target_pairs={{0,4},{1,5},{2,6},{3,7},{4,0},{5,1},{6,2},{7,3},{8,12},{9,13},{10,... | collective-permute-start | bytes 1572872 | tf_op jit(solution)/shard_map/ppermute | solution.py:66
  477.0 23.3 %collective-permute-start.132 = (bf16[384,1024]{1,0:T(8,128)(2,1)S(1)}, bf16[384,1024]{1,0:T(8,128)(2,1)}, u32[]{:S(2)}, u32[]{:S(2)}) collective-permute-start(bf16[384,1024]{1,0:T(8,128)(2,1)S(1)} %fusion.21), channel_id=1, source_target_pairs={{0,8},{8,16},{1,9},{9,17},{2,10},{10,18},{3,11},{11,19},{4,12},{12... | collective-permute-start | bytes 2359304 | tf_op jit(solution)/shard_map/ppermute | solution.py:239
  479.5 18.0 %collective-permute-start.79 = (bf16[256,1024]{1,0:T(8,128)(2,1)}, bf16[256,1024]{1,0:T(8,128)(2,1)}, u32[]{:S(2)}, u32[]{:S(2)}) collective-permute-start(bf16[256,1024]{1,0:T(8,128)(2,1)} %get-tuple-element.96), channel_id=1, source_target_pairs={{0,1},{1,0},{2,3},{3,2},{4,5},{5,4},{6,7},{7,6},{8,9},{9,8},{10,11... | collective-permute-start | bytes 1572872 | tf_op jit(solution)/shard_map/ppermute | solution.py:66
  486.2 18.8 %collective-permute-start.75 = (bf16[256,1024]{1,0:T(8,128)(2,1)}, bf16[256,1024]{1,0:T(8,128)(2,1)S(1)}, u32[]{:S(2)}, u32[]{:S(2)}) collective-permute-start(bf16[256,1024]{1,0:T(8,128)(2,1)} %get-tuple-element.84), channel_id=1, source_target_pairs={{0,1},{1,0},{2,3},{3,2},{4,5},{5,4},{6,7},{7,6},{8,9},{9,8},{10,11... | collective-permute-start | bytes 1572872 | tf_op jit(solution)/shard_map/ppermute | solution.py:66
  486.3 23.3 %collective-permute-start.76 = (bf16[256,1024]{1,0:T(8,128)(2,1)}, bf16[256,1024]{1,0:T(8,128)(2,1)S(1)}, u32[]{:S(2)}, u32[]{:S(2)}) collective-permute-start(bf16[256,1024]{1,0:T(8,128)(2,1)} %get-tuple-element.88), channel_id=1, source_target_pairs={{0,1},{1,0},{2,3},{3,2},{4,5},{5,4},{6,7},{7,6},{8,9},{9,8},{10,11... | collective-permute-start | bytes 1572872 | tf_op jit(solution)/shard_map/ppermute | solution.py:66
  497.4 20.6 %collective-permute-start.78 = (bf16[256,1024]{1,0:T(8,128)(2,1)}, bf16[256,1024]{1,0:T(8,128)(2,1)S(1)}, u32[]{:S(2)}, u32[]{:S(2)}) collective-permute-start(bf16[256,1024]{1,0:T(8,128)(2,1)} %get-tuple-element.92), channel_id=1, source_target_pairs={{0,1},{1,0},{2,3},{3,2},{4,5},{5,4},{6,7},{7,6},{8,9},{9,8},{10,11... | collective-permute-start | bytes 1572872 | tf_op jit(solution)/shard_map/ppermute | solution.py:66
  500.3 21.8 %collective-permute-start.80 = (bf16[256,1024]{1,0:T(8,128)(2,1)}, bf16[256,1024]{1,0:T(8,128)(2,1)S(1)}, u32[]{:S(2)}, u32[]{:S(2)}) collective-permute-start(bf16[256,1024]{1,0:T(8,128)(2,1)} %get-tuple-element.97), channel_id=1, source_target_pairs={{0,2},{1,3},{2,0},{3,1},{4,6},{5,7},{6,4},{7,5},{8,10},{9,11},{10,... | collective-permute-start | bytes 1572872 | tf_op jit(solution)/shard_map/ppermute | solution.py:66
  504.3 21.4 %collective-permute-start.134 = (bf16[384,1024]{1,0:T(8,128)(2,1)S(1)}, bf16[384,1024]{1,0:T(8,128)(2,1)S(1)}, u32[]{:S(2)}, u32[]{:S(2)}) collective-permute-start(bf16[384,1024]{1,0:T(8,128)(2,1)S(1)} %get-tuple-element.135), channel_id=1, source_target_pairs={{24,16},{25,17},{26,18},{27,19},{28,20},{29,21},{30,22},{31,23}} | collective-permute-start | bytes 2359304 | tf_op jit(solution)/shard_map/ppermute | solution.py:240
  505.0 19.3 %collective-permute-start.83 = (bf16[256,1024]{1,0:T(8,128)(2,1)}, bf16[256,1024]{1,0:T(8,128)(2,1)S(1)}, u32[]{:S(2)}, u32[]{:S(2)}) collective-permute-start(bf16[256,1024]{1,0:T(8,128)(2,1)} %get-tuple-element.101), channel_id=1, source_target_pairs={{0,4},{1,5},{2,6},{3,7},{4,0},{5,1},{6,2},{7,3},{8,12},{9,13},{10,... | collective-permute-start | bytes 1572872 | tf_op jit(solution)/shard_map/ppermute | solution.py:66
  509.6 129.3 %collective-permute-start.133 = (bf16[384,1024]{1,0:T(8,128)(2,1)}, bf16[384,1024]{1,0:T(8,128)(2,1)}, u32[]{:S(2)}, u32[]{:S(2)}) collective-permute-start(bf16[384,1024]{1,0:T(8,128)(2,1)} %get-tuple-element.134), channel_id=1, source_target_pairs={{0,8},{8,16},{16,24},{1,9},{9,17},{17,25},{2,10},{10,18},{18,26},{... | collective-permute-start | bytes 2359304 | tf_op jit(solution)/shard_map/ppermute | solution.py:239
  522.1 24.9 %collective-permute-start.82 = (bf16[256,1024]{1,0:T(8,128)(2,1)}, bf16[256,1024]{1,0:T(8,128)(2,1)S(1)}, u32[]{:S(2)}, u32[]{:S(2)}) collective-permute-start(bf16[256,1024]{1,0:T(8,128)(2,1)} %get-tuple-element.99), channel_id=1, source_target_pairs={{0,4},{1,5},{2,6},{3,7},{4,0},{5,1},{6,2},{7,3},{8,12},{9,13},{10,... | collective-permute-start | bytes 1572872 | tf_op jit(solution)/shard_map/ppermute | solution.py:66
  524.3 22.4 %collective-permute-start.81 = (bf16[256,1024]{1,0:T(8,128)(2,1)S(1)}, bf16[256,1024]{1,0:T(8,128)(2,1)S(1)}, u32[]{:S(2)}, u32[]{:S(2)}) collective-permute-start(bf16[256,1024]{1,0:T(8,128)(2,1)S(1)} %add_convert_fusion.11), channel_id=1, source_target_pairs={{0,4},{1,5},{2,6},{3,7},{4,0},{5,1},{6,2},{7,3},{8,12},{9,13},{10,... | collective-permute-start | bytes 1572872 | tf_op jit(solution)/shard_map/ppermute | solution.py:66
  525.7 21.4 %collective-permute-start.84 = (bf16[256,1024]{1,0:T(8,128)(2,1)S(1)}, bf16[256,1024]{1,0:T(8,128)(2,1)S(1)}, u32[]{:S(2)}, u32[]{:S(2)}) collective-permute-start(bf16[256,1024]{1,0:T(8,128)(2,1)S(1)} %add_convert_fusion.9), channel_id=1, source_target_pairs={{0,2},{1,3},{2,0},{3,1},{4,6},{5,7},{6,4},{7,5},{8,10},{9,11},{10,... | collective-permute-start | bytes 1572872 | tf_op jit(solution)/shard_map/ppermute | solution.py:66
  533.2 86.9 %collective-permute-start.135 = (bf16[384,1024]{1,0:T(8,128)(2,1)}, bf16[384,1024]{1,0:T(8,128)(2,1)}, u32[]{:S(2)}, u32[]{:S(2)}) collective-permute-start(bf16[384,1024]{1,0:T(8,128)(2,1)} %fusion.22), channel_id=1, source_target_pairs={{24,16},{16,8},{25,17},{17,9},{26,18},{18,10},{27,19},{19,11},{28,... | collective-permute-start | bytes 2359304 | tf_op jit(solution)/shard_map/ppermute | solution.py:240
  596.4 22.1 %collective-permute-start.113 = (bf16[4,2,2,1,32,1024]{5,4,3,2,1,0:T(8,128)(2,1)S(1)}, bf16[4,2,2,1,32,1024]{5,4,3,2,1,0:T(8,128)(2,1)S(1)}, u32[]{:S(2)}, u32[]{:S(2)}) collective-permute-start(bf16[4,2,2,1,32,1024]{5,4,3,2,1,0:T(8,128)(2,1)S(1)} %constant_dynamic-slice_fusion.5), channel_id=1, source_target_pairs={{0,1},{1,0},{2,3},{3,2},{4,5},{5,4},{6,7},{7,6},{8,9},{9,8},{10,11... | collective-permute-start | bytes 3145736 | tf_op jit(solution)/shard_map/ppermute | solution.py:66
  610.1 35.4 %collective-permute-start.100 = (bf16[4,2,2,1,32,2048]{5,4,3,2,1,0:T(8,128)(2,1)S(1)}, bf16[4,2,2,1,32,2048]{5,4,3,2,1,0:T(8,128)(2,1)S(1)}, u32[]{:S(2)}, u32[]{:S(2)}) collective-permute-start(bf16[4,2,2,1,32,2048]{5,4,3,2,1,0:T(8,128)(2,1)S(1)} %constant_dynamic-slice_fusion.10), channel_id=1, source_target_pairs={{0,1},{1,0},{2,3},{3,2},{4,5},{5,4},{6,7},{7,6},{8,9},{9,8},{10,11... | collective-permute-start | bytes 6291464 | tf_op jit(solution)/shard_map/ppermute | solution.py:66
  621.8 20.3 %collective-permute-start.136 = (bf16[384,1024]{1,0:T(8,128)(2,1)S(1)}, bf16[384,1024]{1,0:T(8,128)(2,1)S(1)}, u32[]{:S(2)}, u32[]{:S(2)}) collective-permute-start(bf16[384,1024]{1,0:T(8,128)(2,1)S(1)} %add_convert_fusion.2), channel_id=1, source_target_pairs={{24,16},{16,8},{8,0},{25,17},{17,9},{9,1},{26,18},{18,10},{10,2},{... | collective-permute-start | bytes 2359304 | tf_op jit(solution)/shard_map/ppermute | solution.py:240
  (212 other events, 3258.8 us)
